TPU v7x, 32 devices: a whole 2x2x4 slice. The times are simulated.
32 devices in a mesh: grp: 2 (over x), samp: 16 (over z, y, core).
Axes of the slice: x: 2, y: 2, z: 4, core: 2. Of those that a mesh axis runs over, the one named last changes fastest.
Arguments:
- tokens: bfloat16 [2, 1536, 8, 512], P('grp', 'samp'), may hold values from -6 to 6
- segments: int32 [2, 1536], P('grp', 'samp'), may hold values from -1 to 3, as said below
- cotangent: bfloat16 [2, 1536, 8, 512], P('grp', 'samp'), may hold values from -6 to 6
- first_gain: float32 [512], replicated, may hold values from 0.1 to 1.9
- first_shift: float32 [512], replicated, may hold values from -3 to 3
- sample_qkv: bfloat16 [512, 1536], replicated, may hold values from -0.25 to 0.25
- sample_out: bfloat16 [512, 512], replicated, may hold values from -0.75 to 0.75
- second_gain: float32 [512], replicated, may hold values from 0.1 to 1.9
- second_shift: float32 [512], replicated, may hold values from -3 to 3
- feature_qkv: bfloat16 [512, 1536], replicated, may hold values from -0.25 to 0.25
- feature_out: bfloat16 [512, 512], replicated, may hold values from -0.75 to 0.75
- third_gain: float32 [512], replicated, may hold values from 0.1 to 1.9
- third_shift: float32 [512], replicated, may hold values from -3 to 3
- up_weight: bfloat16 [512, 2048], replicated, may hold values from -0.25 to 0.25
- up_bias: float32 [2048], replicated, may hold values from -3 to 3
- down_weight: bfloat16 [2048, 512], replicated, may hold values from -0.125 to 0.125
- down_bias: float32 [512], replicated, may hold values from -3 to 3
Outputs:
- output: bfloat16 [2, 1536, 8, 512], P('grp', 'samp')
- grad_tokens: float32 [2, 1536, 8, 512], P('grp', 'samp')
- grad_first_gain: float32 [512], P('samp')
- grad_first_shift: float32 [512], P('samp')
- grad_sample_qkv: float32 [512, 1536], P('samp')
- grad_sample_out: float32 [512, 512], P('samp')
- grad_second_gain: float32 [512], P('samp')
- grad_second_shift: float32 [512], P('samp')
- grad_feature_qkv: float32 [512, 1536], P('samp')
- grad_feature_out: float32 [512, 512], P('samp')
- grad_third_gain: float32 [512], P('samp')
- grad_third_shift: float32 [512], P('samp')
- grad_up_weight: float32 [512, 2048], P('samp')
- grad_up_bias: float32 [2048], P('samp')
- grad_down_weight: float32 [2048, 512], P('samp')
- grad_down_bias: float32 [512], P('samp')
Inputs may be any that keep to these rules, and one draw needn't show every extreme that they name: `segments`: -1 marks a padding slot, other values name a sample's task.
All inputs are finite; a program needn't handle non-finite values.
Results may differ from a plain program's by a relative error of at most 0.023.
Values may be sent and summed in bfloat16 or wider, within the bound.
No kernel may reach another device: no remote copies, remote signals or barrier semaphores. Data moves between devices by JAX's collectives and lax.ppermute only.
A program may use at most 512 MiB of HBM per device.

v0:
```python
import jax
import jax.numpy as jnp
from jax import lax
from jax.sharding import PartitionSpec as P

H = 8
HD = 64


EPSILON = 1e-05
SCALING = 0.125
NEGATIVE = -1e30


def matmul(left, right):
    return jnp.dot(left, right, preferred_element_type=jnp.float32)


def norm_forward(values, gain, shift):
    centre = values - jnp.mean(values, -1, keepdims=True)
    factor = lax.rsqrt(jnp.mean(centre * centre, -1, keepdims=True) + EPSILON)
    normal = centre * factor
    return (normal * gain + shift, normal, factor)


def norm_backward(grad, normal, factor, gain):
    grad_gain = jnp.sum(grad * normal, 0)
    grad_shift = jnp.sum(grad, 0)
    scaled = grad * gain
    grad_values = factor * (
        scaled
        - jnp.mean(scaled, -1, keepdims=True)
        - normal * jnp.mean(scaled * normal, -1, keepdims=True)
    )
    return (grad_values, grad_gain, grad_shift)


def gelu_fn(values):
    return jax.nn.gelu(values, approximate=True)


def body(
    tokens,
    segments,
    cotangent,
    first_gain,
    first_shift,
    sample_qkv,
    sample_out,
    second_gain,
    second_shift,
    feature_qkv,
    feature_out,
    third_gain,
    third_shift,
    up_weight,
    up_bias,
    down_weight,
    down_bias,
):
    count, feats, width = (tokens.shape[1], tokens.shape[2], tokens.shape[3])
    lines = count * feats
    inputs = tokens.reshape(lines, width).astype(jnp.float32)
    seg_local = segments[0]
    first_normed, first_normal, first_factor = norm_forward(inputs, first_gain, first_shift)
    first_low = first_normed.astype(jnp.bfloat16)
    first_proj = matmul(first_low, sample_qkv).astype(jnp.bfloat16)
    query_one = first_proj[:, :width].reshape(count, feats, H, HD)
    key_one = first_proj[:, width : 2 * width].reshape(count, feats, width)
    value_one = first_proj[:, 2 * width :].reshape(count, feats, width)
    keys_all, values_all, seg_all = (
        lax.all_gather(key_one, "samp", axis=0, tiled=True),
        lax.all_gather(value_one, "samp", axis=0, tiled=True),
        lax.all_gather(seg_local.astype(jnp.bfloat16), "samp", axis=0, tiled=True),
    )
    total = seg_all.shape[0]
    offset = lax.axis_index("samp") * count
    own_ids = seg_local.astype(jnp.float32)
    other_ids = seg_all.astype(jnp.float32)
    row_place = offset + lax.broadcasted_iota(jnp.int32, (count, total), 0)
    col_place = lax.broadcasted_iota(jnp.int32, (count, total), 1)
    allowed = (own_ids[:, None] == other_ids[None, :]) & (other_ids[None, :] >= 0.0) | (
        row_place == col_place
    )

    def sample_scores(keys_whole):
        raw = (
            jnp.einsum(
                "ifhd,jfhd->fhij",
                query_one,
                keys_whole.reshape(total, feats, H, HD),
                preferred_element_type=jnp.float32,
            )
            * SCALING
        )
        return jnp.where(allowed, raw, NEGATIVE)

    scores_one = sample_scores(keys_all)
    top_one = jnp.max(scores_one, -1, keepdims=True)
    expo_one = jnp.exp(scores_one - top_one)
    total_one = jnp.sum(expo_one, -1, keepdims=True)
    probs_one = expo_one / total_one
    log_total = top_one + jnp.log(total_one)
    mixed_one = jnp.einsum(
        "fhij,jfhd->ifhd",
        probs_one.astype(jnp.bfloat16),
        values_all.reshape(total, feats, H, HD),
        preferred_element_type=jnp.float32,
    )
    first_attn = mixed_one.reshape(lines, width).astype(jnp.bfloat16)
    after_first = inputs + matmul(first_attn, sample_out)
    second_normed, second_normal, second_factor = norm_forward(
        after_first, second_gain, second_shift
    )
    second_low = second_normed.astype(jnp.bfloat16)
    second_proj = matmul(second_low, feature_qkv).astype(jnp.bfloat16)
    query_two = second_proj[:, :width].reshape(count, feats, H, HD)
    key_two = second_proj[:, width : 2 * width].reshape(count, feats, H, HD)
    value_two = second_proj[:, 2 * width :].reshape(count, feats, H, HD)
    scores_two = (
        jnp.einsum("ifhd,ighd->ihfg", query_two, key_two, preferred_element_type=jnp.float32)
        * SCALING
    )
    expo_two = jnp.exp(scores_two - jnp.max(scores_two, -1, keepdims=True))
    probs_two = expo_two / jnp.sum(expo_two, -1, keepdims=True)
    probs_two_low = probs_two.astype(jnp.bfloat16)
    mixed_two = jnp.einsum(
        "ihfg,ighd->ifhd", probs_two_low, value_two, preferred_element_type=jnp.float32
    )
    second_attn = mixed_two.reshape(lines, width).astype(jnp.bfloat16)
    after_second = after_first + matmul(second_attn, feature_out)
    third_normed, third_normal, third_factor = norm_forward(after_second, third_gain, third_shift)
    third_low = third_normed.astype(jnp.bfloat16)
    hidden_pre = matmul(third_low, up_weight) + up_bias
    hidden_low = gelu_fn(hidden_pre).astype(jnp.bfloat16)
    result = after_second + matmul(hidden_low, down_weight) + down_bias
    grad_result = cotangent.reshape(lines, width).astype(jnp.float32)
    down_grad = grad_result.astype(jnp.bfloat16)
    grad_down_bias = jnp.sum(down_grad.astype(jnp.float32), 0)
    grad_down_weight = matmul(hidden_low.T, down_grad)
    grad_hidden = matmul(down_grad, down_weight.T)
    gelu_pull = jax.vjp(gelu_fn, hidden_pre)[1]
    pre_grad = gelu_pull(grad_hidden)[0].astype(jnp.bfloat16)
    grad_up_bias = jnp.sum(pre_grad.astype(jnp.float32), 0)
    grad_up_weight = matmul(third_low.T, pre_grad)
    third_back, grad_third_gain, grad_third_shift = norm_backward(
        matmul(pre_grad, up_weight.T), third_normal, third_factor, third_gain
    )
    grad_second = grad_result + third_back
    attn_grad_two = grad_second.astype(jnp.bfloat16)
    grad_feature_out = matmul(second_attn.T, attn_grad_two)
    mixed_grad_two = (
        matmul(attn_grad_two, feature_out.T).astype(jnp.bfloat16).reshape(count, feats, H, HD)
    )
    prob_grad_two = jnp.einsum(
        "ifhd,ighd->ihfg", mixed_grad_two, value_two, preferred_element_type=jnp.float32
    )
    value_grad_two = jnp.einsum(
        "ihfg,ifhd->ighd", probs_two_low, mixed_grad_two, preferred_element_type=jnp.float32
    )
    score_grad_two = (
        probs_two * (prob_grad_two - jnp.sum(probs_two * prob_grad_two, -1, keepdims=True))
    ).astype(jnp.bfloat16)
    query_grad_two = (
        jnp.einsum("ihfg,ighd->ifhd", score_grad_two, key_two, preferred_element_type=jnp.float32)
        * SCALING
    )
    key_grad_two = (
        jnp.einsum("ihfg,ifhd->ighd", score_grad_two, query_two, preferred_element_type=jnp.float32)
        * SCALING
    )
    proj_grad_two = jnp.concatenate(
        [
            query_grad_two.reshape(lines, width),
            key_grad_two.reshape(lines, width),
            value_grad_two.reshape(lines, width),
        ],
        -1,
    ).astype(jnp.bfloat16)
    grad_feature_qkv = matmul(second_low.T, proj_grad_two)
    second_back, grad_second_gain, grad_second_shift = norm_backward(
        matmul(proj_grad_two, feature_qkv.T), second_normal, second_factor, second_gain
    )
    grad_first = grad_second + second_back
    upper = (
        grad_second_gain,
        grad_second_shift,
        grad_feature_qkv,
        grad_feature_out,
        grad_third_gain,
        grad_third_shift,
        grad_up_weight,
        grad_up_bias,
        grad_down_weight,
        grad_down_bias,
    )
    attn_grad_one = grad_first.astype(jnp.bfloat16)
    grad_sample_out = matmul(first_attn.T, attn_grad_one)
    mixed_grad_one = (
        matmul(attn_grad_one, sample_out.T).astype(jnp.bfloat16).reshape(count, feats, H, HD)
    )
    keys_back, values_back = (
        lax.all_gather(key_one, "samp", axis=0, tiled=True),
        lax.all_gather(value_one, "samp", axis=0, tiled=True),
    )
    probs_back = jnp.exp(sample_scores(keys_back) - log_total)
    prob_grad_one = jnp.einsum(
        "ifhd,jfhd->fhij",
        mixed_grad_one,
        values_back.reshape(total, feats, H, HD),
        preferred_element_type=jnp.float32,
    )
    row_dots = jnp.sum(probs_back * prob_grad_one, -1, keepdims=True)
    score_grad_one = (probs_back * (prob_grad_one - row_dots)).astype(jnp.bfloat16)
    query_grad_one = (
        jnp.einsum(
            "fhij,jfhd->ifhd",
            score_grad_one,
            keys_back.reshape(total, feats, H, HD),
            preferred_element_type=jnp.float32,
        )
        * SCALING
    )
    grads_all, queries_all = (
        lax.all_gather(mixed_grad_one, "samp", axis=0, tiled=True),
        lax.all_gather(query_one, "samp", axis=0, tiled=True),
    )
    lse_all, dots_all = (
        lax.all_gather(log_total, "samp", axis=2, tiled=True),
        lax.all_gather(row_dots, "samp", axis=2, tiled=True),
    )
    col_ids = own_ids[:, None]
    row_ids = other_ids[None, :]
    allowed_cols = (col_ids == row_ids) & (col_ids >= 0.0) | (row_place == col_place)
    raw_cols = (
        jnp.einsum(
            "jfhd,ifhd->fhji",
            key_one.reshape(count, feats, H, HD),
            queries_all,
            preferred_element_type=jnp.float32,
        )
        * SCALING
    )
    scores_cols = jnp.where(allowed_cols, raw_cols, NEGATIVE)
    probs_cols = jnp.exp(scores_cols - jnp.swapaxes(lse_all, 2, 3))
    dots_cols = jnp.einsum(
        "jfhd,ifhd->fhji",
        value_one.reshape(count, feats, H, HD),
        grads_all,
        preferred_element_type=jnp.float32,
    )
    score_cols = (probs_cols * (dots_cols - jnp.swapaxes(dots_all, 2, 3))).astype(jnp.bfloat16)
    key_grad_one = (
        jnp.einsum("fhji,ifhd->jfhd", score_cols, queries_all, preferred_element_type=jnp.float32)
        * SCALING
    )
    value_grad_one = jnp.einsum(
        "fhji,ifhd->jfhd",
        probs_cols.astype(jnp.bfloat16),
        grads_all,
        preferred_element_type=jnp.float32,
    )
    proj_grad_one = jnp.concatenate(
        [
            query_grad_one.reshape(lines, width),
            key_grad_one.reshape(lines, width),
            value_grad_one.reshape(lines, width),
        ],
        -1,
    ).astype(jnp.bfloat16)
    grad_sample_qkv = matmul(first_low.T, proj_grad_one)
    first_back, grad_first_gain, grad_first_shift = norm_backward(
        matmul(proj_grad_one, sample_qkv.T), first_normal, first_factor, first_gain
    )
    grad_inputs = grad_first + first_back
    summed = (
        lax.psum_scatter(
            grad_first_gain.astype(jnp.bfloat16), "samp", scatter_dimension=0, tiled=True
        ).astype(jnp.float32),
        lax.psum_scatter(
            grad_first_shift.astype(jnp.bfloat16), "samp", scatter_dimension=0, tiled=True
        ).astype(jnp.float32),
        lax.psum_scatter(
            grad_sample_qkv.astype(jnp.bfloat16), "samp", scatter_dimension=0, tiled=True
        ).astype(jnp.float32),
        lax.psum_scatter(
            grad_sample_out.astype(jnp.bfloat16), "samp", scatter_dimension=0, tiled=True
        ).astype(jnp.float32),
        lax.psum_scatter(
            upper[0].astype(jnp.bfloat16), "samp", scatter_dimension=0, tiled=True
        ).astype(jnp.float32),
        lax.psum_scatter(
            upper[1].astype(jnp.bfloat16), "samp", scatter_dimension=0, tiled=True
        ).astype(jnp.float32),
        lax.psum_scatter(
            upper[2].astype(jnp.bfloat16), "samp", scatter_dimension=0, tiled=True
        ).astype(jnp.float32),
        lax.psum_scatter(
            upper[3].astype(jnp.bfloat16), "samp", scatter_dimension=0, tiled=True
        ).astype(jnp.float32),
        lax.psum_scatter(
            upper[4].astype(jnp.bfloat16), "samp", scatter_dimension=0, tiled=True
        ).astype(jnp.float32),
        lax.psum_scatter(
            upper[5].astype(jnp.bfloat16), "samp", scatter_dimension=0, tiled=True
        ).astype(jnp.float32),
        lax.psum_scatter(
            upper[6].astype(jnp.bfloat16), "samp", scatter_dimension=0, tiled=True
        ).astype(jnp.float32),
        lax.psum_scatter(
            upper[7].astype(jnp.bfloat16), "samp", scatter_dimension=0, tiled=True
        ).astype(jnp.float32),
        lax.psum_scatter(
            upper[8].astype(jnp.bfloat16), "samp", scatter_dimension=0, tiled=True
        ).astype(jnp.float32),
        lax.psum_scatter(
            upper[9].astype(jnp.bfloat16), "samp", scatter_dimension=0, tiled=True
        ).astype(jnp.float32),
    )
    summed = (
        lax.psum(summed[0].astype(jnp.bfloat16), "grp").astype(jnp.float32),
        lax.psum(summed[1].astype(jnp.bfloat16), "grp").astype(jnp.float32),
        lax.psum(summed[2].astype(jnp.bfloat16), "grp").astype(jnp.float32),
        lax.psum(summed[3].astype(jnp.bfloat16), "grp").astype(jnp.float32),
        lax.psum(summed[4].astype(jnp.bfloat16), "grp").astype(jnp.float32),
        lax.psum(summed[5].astype(jnp.bfloat16), "grp").astype(jnp.float32),
        lax.psum(summed[6].astype(jnp.bfloat16), "grp").astype(jnp.float32),
        lax.psum(summed[7].astype(jnp.bfloat16), "grp").astype(jnp.float32),
        lax.psum(summed[8].astype(jnp.bfloat16), "grp").astype(jnp.float32),
        lax.psum(summed[9].astype(jnp.bfloat16), "grp").astype(jnp.float32),
        lax.psum(summed[10].astype(jnp.bfloat16), "grp").astype(jnp.float32),
        lax.psum(summed[11].astype(jnp.bfloat16), "grp").astype(jnp.float32),
        lax.psum(summed[12].astype(jnp.bfloat16), "grp").astype(jnp.float32),
        lax.psum(summed[13].astype(jnp.bfloat16), "grp").astype(jnp.float32),
    )
    output = result.astype(jnp.bfloat16).reshape(1, count, feats, width)
    grad_tokens = grad_inputs.reshape(1, count, feats, width)
    return (
        output,
        grad_tokens,
        summed[0],
        summed[1],
        summed[2],
        summed[3],
        summed[4],
        summed[5],
        summed[6],
        summed[7],
        summed[8],
        summed[9],
        summed[10],
        summed[11],
        summed[12],
        summed[13],
    )


def solution(mesh):
    in_specs = (
        P("grp", "samp", None, None),
        P("grp", "samp"),
        P("grp", "samp", None, None),
        P(),
        P(),
        P(),
        P(),
        P(),
        P(),
        P(),
        P(),
        P(),
        P(),
        P(),
        P(),
        P(),
        P(),
    )
    out_specs = (
        P("grp", "samp", None, None),
        P("grp", "samp", None, None),
        P("samp"),
        P("samp"),
        P("samp", None),
        P("samp", None),
        P("samp"),
        P("samp"),
        P("samp", None),
        P("samp", None),
        P("samp"),
        P("samp"),
        P("samp", None),
        P("samp"),
        P("samp", None),
        P("samp"),
    )
    return jax.shard_map(body, mesh=mesh, in_specs=in_specs, out_specs=out_specs, check_vma=False)
```

profile of v0, /device:TPU:0, one launch (start us, length us, event | category | flops | bytes accessed | tf_op | source)
XLA Modules:
  0.0 1040.8 jit_solution(10730719580633782035)
XLA Ops:
  20.6 36.5 %all-reduce = bf16[1536]{0:T(1024)(128)(2,1)S(1)} all-reduce(bf16[1536]{0:T(1024)(128)(2,1)S(1)} %dynamic-update-slice), channel_id=2, replica_groups=mesh['grp'=2,'samp'=16] {'samp'}, use_global_device_ids=true, to_apply=%add | all-reduce | flops 1536 | bytes 6144
  58.2 62.2 %all-gather.8.cloned.1.call-done = bf16[1536,8,512]{2,1,0:T(8,128)(2,1)} async-done(((bf16[96,8,512]{2,1,0:T(8,128)(2,1)}), bf16[1536,8,512]{2,1,0:T(8,128)(2,1)}) %all-gather.8.cloned.1.call-update) | async-done | bytes 12582928 | tf_op jit(solution)/shard_map/all_gather | solution.py:73
  120.4 16.9 %copy.109 = bf16[1536,8,512]{0,2,1:T(8,128)(2,1)} copy(bf16[1536,8,512]{2,1,0:T(8,128)(2,1)} %all-gather.8.cloned.1.call-done) | data formatting | bytes 25165824 | tf_op jit(solution)/shard_map/all_gather | solution.py:73
  137.3 84.4 %all-gather.10.cloned.1.call-done = bf16[1536,8,512]{2,1,0:T(8,128)(2,1)} async-done(((bf16[96,8,512]{2,1,0:T(8,128)(2,1)}), bf16[1536,8,512]{2,1,0:T(8,128)(2,1)}) %all-gather.10.cloned.1.call-update) | async-done | bytes 12582928 | tf_op jit(solution)/shard_map/all_gather | solution.py:72
  221.7 17.0 %copy.110 = bf16[1536,8,512]{0,2,1:T(8,128)(2,1)} copy(bf16[1536,8,512]{2,1,0:T(8,128)(2,1)} %all-gather.10.cloned.1.call-done) | data formatting | bytes 25165824 | tf_op jit(solution)/shard_map/all_gather | solution.py:72
  238.7 21.1 %fusion.3 = (f32[8,8,96]{2,1,0:T(8,128)S(1)}, f32[8,8,96,1536]{3,2,1,0:T(8,128)}) fusion(pred[96,1536]{1,0:T(8,128)(4,1)S(1)} %get-tuple-element.59, bf16[1536,8,8,64]{0,3,2,1:T(8,128)(2,1)} %bitcast.124, bf16[96,8,8,64]{3,2,1,0:T(8,128)(2,1)} %reshape.238), kind=kOutput, calls=%fused_computation.11 | convolution fusion | flops 1236264960 | bytes 51290112 | tf_op jit(solution)/shard_map/ifhd,jfhd->fhij/dot_general | solution.py:88
  259.8 16.9 %fusion.1 = f32[8,8,96]{2,1,0:T(8,128)S(1)} fusion(f32[8,8,96,1536]{3,2,1,0:T(8,128)} %get-tuple-element.65, f32[8,8,96]{2,1,0:T(8,128)S(1)} %get-tuple-element.64, pred[96,1536]{1,0:T(8,128)(4,1)S(1)} %get-tuple-element.59), kind=kLoop, calls=%fused_computation.9 | loop fusion | flops 37742592 | bytes 37945344 | tf_op jit(solution)/shard_map/reduce_sum | solution.py:101
  277.3 20.6 %fusion.74 = bf16[96,8,8,64]{0,3,2,1:T(8,128)(2,1)} fusion(bf16[1536,8,8,64]{0,3,2,1:T(8,128)(2,1)} %bitcast.126, f32[8,8,96,1536]{3,2,1,0:T(8,128)} %get-tuple-element.65, f32[8,8,96]{2,1,0:T(8,128)S(1)} %fusion.1, f32[8,8,96]{2,1,0:T(8,128)S(1)} %get-tuple-element.64, pred[96,1536]{1,0:T(8,128)(4,1)S(1)} %get-tuple-element.59), kind=kOutput, calls=%fused_computation.115 | convolution fusion | flops 1255538688 | bytes 51314688 | tf_op jit(solution)/shard_map/fhij,jfhd->ifhd/dot_general | solution.py:104
  322.5 22.0 %fusion.106 = (f32[96,8,8]{2,1,0:T(8,128)S(1)}, f32[96,8,8,8]{2,3,1,0:T(8,128)S(1)}) fusion(f32[96,8,8,8]{2,3,1,0:T(8,128)S(1)} %fusion.67), kind=kOutput, calls=%fused_computation.174 | output fusion | flops 196615 | bytes 417792 | tf_op jit(solution)/shard_map/sub | solution.py:124
  416.7 31.3 %multiply_reduce_fusion = (f32[8,8,96]{2,1,0:T(8,128)S(1)}, f32[8,8,96,1536]{3,2,1,0:T(8,128)}) fusion(f32[8,8,96,1536]{3,2,1,0:T(8,128)} %get-tuple-element.65, f32[8,8,96]{2,1,0:T(8,128)S(1)} %log_add_fusion, pred[96,1536]{1,0:T(8,128)(4,1)S(1)} %get-tuple-element.59, bf16[1536,8,8,64]{0,3,2,1:T(8,128)(2,1)} %bitcast.127, bf16[96,8,8,64]{3,2,1,0:T(8,128)(2,1)} %reshape.250), kind=kOutput, calls=%fused_computation.4 | convolution fusion | flops 1255139328 | bytes 89063424 | tf_op jit(solution)/shard_map/ifhd,jfhd->fhij/dot_general | solution.py:207
  452.5 31.4 %fusion.78 = bf16[96,8,8,64]{0,3,2,1:T(8,128)(2,1)S(1)} fusion(bf16[1536,8,8,64]{0,3,2,1:T(8,128)(2,1)} %bitcast.125, f32[8,8,96,1536]{3,2,1,0:T(8,128)} %get-tuple-element.77, f32[8,8,96,1536]{3,2,1,0:T(8,128)} %get-tuple-element.65, f32[8,8,96]{2,1,0:T(8,128)S(1)} %get-tuple-element.76, f32[8,8,96]{2,1,0:T(8,128)S(1)} %log_add_fusion, ...), kind=kOutput, calls=%fused_computation.117 | convolution fusion | flops 1265369088 | bytes 89063424 | tf_op jit(solution)/shard_map/fhij,jfhd->ifhd/dot_general | solution.py:216
  489.1 101.6 %all-gather.2 = f32[8,8,1536]{1,0,2:T(8,128)} all-gather(f32[8,8,96]{1,0,2:T(8,128)S(1)} %copy-done.25), channel_id=4, replica_groups=mesh['grp'=2,'samp'=16] {'samp'}, dimensions={2}, use_global_device_ids=true | all-gather | bytes 417792 | tf_op jit(solution)/shard_map/all_gather | solution.py:230
  595.0 72.8 %all-gather.1 = f32[8,8,1536]{1,0,2:T(8,128)} all-gather(f32[8,8,96]{1,0,2:T(8,128)S(1)} %copy.131), channel_id=3, replica_groups=mesh['grp'=2,'samp'=16] {'samp'}, dimensions={2}, use_global_device_ids=true | all-gather | bytes 417792 | tf_op jit(solution)/shard_map/all_gather | solution.py:229
  677.8 27.0 %copy.137 = bf16[1536,8,8,64]{0,3,2,1:T(8,128)(2,1)} copy(bf16[1536,8,8,64]{3,2,1,0:T(8,128)(2,1)} %all-gather.12.cloned.1.call-done) | data formatting | bytes 25165824 | tf_op jit(solution)/shard_map/all_gather | solution.py:226
  706.9 7.3 convolution_convert_fusion.2
  714.2 18.8 %fusion.46 = f32[8,8,96,1536]{3,2,1,0:T(8,128)} fusion(bf16[1536,8,8,64]{0,3,2,1:T(8,128)(2,1)} %copy.137, bf16[96,8,8,64]{3,2,1,0:T(8,128)(2,1)} %reshape_reshape.6), kind=kOutput, calls=%fused_computation.71 | convolution fusion | flops 1207959552 | bytes 51118080 | tf_op jit(solution)/shard_map/jfhd,ifhd->fhji/dot_general | solution.py:236
  733.1 27.2 %copy.134 = bf16[1536,8,8,64]{0,3,2,1:T(8,128)(2,1)} copy(bf16[1536,8,8,64]{3,2,1,0:T(8,128)(2,1)} %all-gather.14.cloned.1.call-done) | data formatting | bytes 25165824 | tf_op jit(solution)/shard_map/all_gather | solution.py:225
  760.3 25.7 %fusion.71 = bf16[96,8,8,64]{0,3,2,1:T(8,128)(2,1)S(1)} fusion(bf16[1536,8,8,64]{0,3,2,1:T(8,128)(2,1)} %copy.137, f32[8,8,96,1536]{3,2,1,0:T(8,128)} %fusion.46, f32[8,8,1536]{2,1,0:T(8,128)S(1)} %copy.136, f32[8,8,1536]{2,1,0:T(8,128)S(1)} %copy.132, pred[96,1536]{1,0:T(8,128)(4,1)} %get-tuple-element.58, bf16[1536,8,8,64]{0,3,2,1:T(8,128)(2,1)} %copy.134, ...), kind=kOutput, calls=%fused_computation.114 | convolution fusion | flops 2473328640 | bytes 65421312 | tf_op jit(solution)/shard_map/fhji,ifhd->jfhd/dot_general | solution.py:254
  792.5 19.9 %fusion.75 = bf16[96,8,8,64]{0,3,2,1:T(8,128)(2,1)S(1)} fusion(bf16[1536,8,8,64]{0,3,2,1:T(8,128)(2,1)} %copy.134, f32[8,8,96,1536]{3,2,1,0:T(8,128)} %fusion.46, f32[8,8,1536]{2,1,0:T(8,128)S(1)} %copy.132, pred[96,1536]{1,0:T(8,128)(4,1)S(1)} %copy-done.36), kind=kOutput, calls=%fused_computation.116 | convolution fusion | flops 1246101504 | bytes 51658752 | tf_op jit(solution)/shard_map/fhji,ifhd->jfhd/dot_general | solution.py:257
  829.5 7.0 fusion.79
  839.4 61.3 %all-reduce.9 = (bf16[512]{0:T(512)(128)(2,1)S(1)}, bf16[512]{0:T(512)(128)(2,1)S(1)}, bf16[512]{0:T(512)(128)(2,1)S(1)}, bf16[512]{0:T(512)(128)(2,1)S(1)}, bf1...) all-reduce(bf16[512]{0:T(512)(128)(2,1)S(1)} %get-tuple-element.20,, ...), channel_id=5, replica_groups=mesh['grp'=2,'samp'=16] {'samp'}, use_global_device_ids=true, to_apply=%region_19.20.clone | all-reduce | flops 5632 | bytes 22528
  908.5 63.0 %reduce-scatter.7.cloned.1.call-done = bf16[32,1536]{1,0:T(8,128)(2,1)} async-done(((bf16[512,1536]{1,0:T(8,128)(2,1)}), bf16[32,1536]{1,0:T(8,128)(2,1)}) %reduce-scatter.7.cloned.1.call-update) | async-done | bytes 98320 | tf_op jit(solution)/shard_map/reduce_scatter | solution.py:283
  975.3 21.0 %all-reduce.15.cloned.1.call-done = (bf16[32]{0:T(256)(128)(2,1)}, bf16[32]{0:T(256)(128)(2,1)}, bf16[32,512]{1,0:T(8,128)(2,1)}, bf16[32]{0:T(256)(128)(2,1)}, ...) async-done(((bf16[32]{0:T(256)(128)(2,1)}, ...) | async-done | bytes 66256 | tf_op jit(solution)/shard_map/psum | solution.py:321
  1008.2 19.1 %all-reduce.17.cloned.1.call-done = (bf16[32,1536]{1,0:T(8,128)(2,1)}, bf16[32,1536]{1,0:T(8,128)(2,1)}, bf16[32,2048]{1,0:T(8,128)(2,1)}, bf16[128,512]{1,0:T(8,128)(2,1)}) async-done(((bf16[32,1536]{1,0:T(8,128)(2,1)}, bf16[32,1536]{1,0:T(8,128)(2,1)}, bf16[32,2048]{1,0:T(8,128)(2,1)}, bf16[128,512]{1,0:T(8,128)(2,1)}), (bf16[32,1536]{1,0:T(8,128)(2,1)}, bf16[32,1536]{1,0:T(8,128)(2,1)}, ...) | async-done | bytes 458768 | tf_op jit(solution)/shard_map/psum | solution.py:323
  (287 shorter events, 191.4 us)
Async XLA Ops:
  7.2 345.9 %copy-start = (bf16[512,2048]{1,0:T(8,128)(2,1)S(1)}, bf16[512,2048]{1,0:T(8,128)(2,1)}, u32[]{:S(2)}) copy-start(bf16[512,2048]{1,0:T(8,128)(2,1)} %param.30) | copy-start | bytes 6291460
  7.2 113.2 %all-gather.8.cloned.1.call-start = ((), (), s32[]{:S(2)}) async-start(), calls=%async_computation.6 | async-start | bytes 13369344 | tf_op jit(solution)/shard_map/all_gather | solution.py:73
  16.5 205.2 %all-gather.10.cloned.1.call-start = ((), (), s32[]{:S(2)}) async-start(), calls=%async_computation.7 | async-start | bytes 13369344 | tf_op jit(solution)/shard_map/all_gather | solution.py:72
  17.3 660.5 %all-gather.12.cloned.1.call-start = ((), (), s32[]{:S(2)}) async-start(), calls=%async_computation.8 | async-start | bytes 26738688 | tf_op jit(solution)/shard_map/all_gather | solution.py:226
  19.0 714.1 %all-gather.14.cloned.1.call-start = ((), (), s32[]{:S(2)}) async-start(), calls=%async_computation.9 | async-start | bytes 26738688 | tf_op jit(solution)/shard_map/all_gather | solution.py:225
  259.8 16.9 %copy-start.28 = (f32[8,8,96]{2,1,0:T(8,128)}, f32[8,8,96]{2,1,0:T(8,128)S(1)}, u32[]{:S(2)}) copy-start(f32[8,8,96]{2,1,0:T(8,128)S(1)} %get-tuple-element.64) | copy-start | bytes 73732
  297.9 8.1 copy-start.12
  297.9 8.1 copy-start.22
  322.5 22.0 %copy-start.24 = (bf16[96,8,8,64]{3,2,1,0:T(8,128)(2,1)S(1)}, bf16[96,8,8,64]{3,2,1,0:T(8,128)(2,1)}, u32[]{:S(2)}) copy-start(bf16[96,8,8,64]{3,2,1,0:T(8,128)(2,1)} %reshape.241) | copy-start | bytes 2359300
  352.7 11.7 %copy-start.5 = (f32[768,512]{1,0:T(8,128)}, f32[768,512]{1,0:T(8,128)S(1)}, u32[]{:S(2)}) copy-start(f32[768,512]{1,0:T(8,128)S(1)} %get-tuple-element.71) | copy-start | bytes 4718596
  352.8 11.7 %copy-start.32 = (f32[768]{0:T(1024)}, f32[768]{0:T(1024)S(1)}, u32[]{:S(2)}) copy-start(f32[768]{0:T(1024)S(1)} %broadcast_multiply_fusion.7) | copy-start | bytes 9220
  353.1 11.3 %copy-start.34 = (f32[768]{0:T(1024)}, f32[768]{0:T(1024)S(1)}, u32[]{:S(2)}) copy-start(f32[768]{0:T(1024)S(1)} %add_rsqrt_fusion.1) | copy-start | bytes 9220
  404.2 501.1 %reduce-scatter.9.cloned.1.call-start = ((), (), s32[]{:S(2)}) async-start(), calls=%async_computation.11 | async-start | bytes 557056 | tf_op jit(solution)/shard_map/reduce_scatter | solution.py:286
  407.3 498.0 %reduce-scatter.13.cloned.1.call-start = ((), (), s32[]{:S(2)}) async-start(), calls=%async_computation.13 | async-start | bytes 557056 | tf_op jit(solution)/shard_map/reduce_scatter | solution.py:298
  416.7 31.4 %copy-start.67 = (f32[512]{0:T(512)S(1)}, f32[512]{0:T(512)}, u32[]{:S(2)}) copy-start(f32[512]{0:T(512)} %param.25) | copy-start | bytes 6148
  416.7 488.7 %reduce-scatter.11.cloned.1.call-start = ((), (), s32[]{:S(2)}) async-start(), calls=%async_computation.12 | async-start | bytes 1671168 | tf_op jit(solution)/shard_map/reduce_scatter | solution.py:295
  452.5 453.0 %reduce-scatter.15.cloned.1.call-start = ((), (), s32[]{:S(2)}) async-start(), calls=%async_computation.14 | async-start | bytes 2228224 | tf_op jit(solution)/shard_map/reduce_scatter | solution.py:307
  677.7 29.2 %copy-start.17 = (bf16[1,96,8,512]{3,2,1,0:T(8,128)(2,1)S(1)}, bf16[1,96,8,512]{3,2,1,0:T(8,128)(2,1)}, u32[]{:S(2)}) copy-start(bf16[1,96,8,512]{3,2,1,0:T(8,128)(2,1)} %param.19) | copy-start | bytes 2359300
  677.7 29.2 %copy-start.65 = (f32[2048]{0:T(1024)S(1)}, f32[2048]{0:T(1024)}, u32[]{:S(2)}) copy-start(f32[2048]{0:T(1024)} %param.31) | copy-start | bytes 24580
  677.7 230.8 %reduce-scatter.17.cloned.1.call-start = ((), (), s32[]{:S(2)}) async-start(), calls=%async_computation.15 | async-start | bytes 2228224 | tf_op jit(solution)/shard_map/reduce_scatter | solution.py:313
  733.0 238.5 %reduce-scatter.7.cloned.1.call-start = ((), (), s32[]{:S(2)}) async-start(), calls=%async_computation.10 | async-start | bytes 1671168 | tf_op jit(solution)/shard_map/reduce_scatter | solution.py:283
  826.9 169.4 %all-reduce.15.cloned.1.call-start = ((), (), s32[]{:S(2)}) async-start(), calls=%async_computation.16 | async-start | bytes 139264 | tf_op jit(solution)/shard_map/psum | solution.py:321
  905.3 121.9 %all-reduce.17.cloned.1.call-start = ((), (), s32[]{:S(2)}) async-start(), calls=%async_computation.17 | async-start | bytes 917504 | tf_op jit(solution)/shard_map/psum | solution.py:323
  971.6 62.1 %copy-start.1 = (bf16[512,2048]{1,0:T(8,128)(2,1)S(1)}, bf16[512,2048]{1,0:T(8,128)(2,1)}, u32[]{:S(2)}) copy-start(bf16[512,2048]{1,0:T(8,128)(2,1)} %param.30) | copy-start | bytes 6291460
  (60 other events, 184.6 us)
Sparse Core Ops, SparseCore 0:
  16.6 103.7 all-gather.7
  122.7 98.9 all-gather.9
  223.8 126.7 all-gather.11
  404.3 177.3 all-gather.13
  585.1 72.4 reduce-scatter.8
  661.4 55.4 reduce-scatter.12
  720.5 58.5 reduce-scatter.10
  783.3 60.6 reduce-scatter.14
  847.7 60.7 reduce-scatter.16
  913.0 58.4 reduce-scatter.6
  975.5 20.6 all-reduce.14
  998.6 28.6 all-reduce.16
where the time goes:
time: 1050 us; the launch traced here: 1040 us
  blocking collectives  272 us (26%)
  waiting for transfers between devices  254 us (24%)
  matrix products  246 us (23%)
  local copies, waits for them, and re-layouts  181 us (17%)
  other arithmetic  69.2 us (7%)
  between operations  17.6 us (2%)
    all_gather x1, blocking collectives, body(): lax.all_gather(row_dots, 'samp', axis=2, tiled=True)  102 us
    unnamed x2, blocking collectives  97.8 us
    all_gather x1, waiting for transfers between devices, body(): lax.all_gather(key_one, 'samp', axis=0, tiled=True)  84.4 us
    all_gather x1, blocking collectives, body(): lax.all_gather(log_total, 'samp', axis=2, tiled=True)  72.8 us
    reduce_scatter x1, waiting for transfers between devices, body(): lax.psum_scatter(grad_sample_qkv.astype(jnp.bfloat16), 'samp', scatter_di...  63 us
    all_gather x1, waiting for transfers between devices, body(): lax.all_gather(value_one, 'samp', axis=0, tiled=True)  62.2 us
    dot_general x18, matrix products, matmul(): return jnp.dot(left, right, preferred_element_type=jnp.float32)  62.1 us
    dot_general x1, matrix products, body(): jnp.einsum('fhij,jfhd->ifhd', score_grad_one, keys_back.reshape(total, fe...  31.4 us
  transfers between devices with their start and end apart: 12, of which 6 were waited for; matrix products, arithmetic and copies ran while one was open for 46% of the time, Pallas kernels for 0%

commit v1 on v0

v1 whole, which is shorter than its diff:
```python
import functools
import math

import jax
import jax.numpy as jnp
from jax import lax
from jax.experimental import pallas as pl
from jax.experimental.pallas import tpu as pltpu
from jax.sharding import PartitionSpec as P

H = 8
HD = 64
EPSILON = 1e-05
SCALING = 0.125
NEGATIVE = -1e30
BF = jnp.bfloat16
F32 = jnp.float32
TILE = 256
LANES = 128
PAD = 8
GELU_C = math.sqrt(2.0 / math.pi)
GELU_A = 0.044715
VMEM_LIMIT = 60 * 1024 * 1024
CLASSES = 5


def dot(a, b):
    return jnp.dot(a, b, preferred_element_type=F32)


def dot_nt(a, b):
    return lax.dot_general(a, b, (((1,), (1,)), ((), ())), preferred_element_type=F32)


def dot_tn(a, b):
    return lax.dot_general(a, b, (((0,), (0,)), ((), ())), preferred_element_type=F32)


def ln_parts(v):
    c = v - jnp.mean(v, -1, keepdims=True)
    r = lax.rsqrt(jnp.mean(c * c, -1, keepdims=True) + EPSILON)
    return c * r, r


def ln_back(dh, n, r, g):
    e = dh * g
    return r * (e - jnp.mean(e, -1, keepdims=True) - n * jnp.mean(e * n, -1, keepdims=True))


def flip(v):
    return jnp.transpose(v)


def lay(scr, v):
    for a in range(scr.shape[0]):
        scr[a] = v[:, a * LANES : (a + 1) * LANES]


def lift(scr):
    return jnp.concatenate([scr[a] for a in range(scr.shape[0])], -1)


def take(scr, first, count, step):
    return jnp.concatenate(
        [scr[a, pl.ds(first, count, stride=step), :] for a in range(scr.shape[0])], -1
    )


def place(scr, first, count, step, v):
    for a in range(scr.shape[0]):
        scr[a, pl.ds(first, count, stride=step), :] = v[:, a * LANES : (a + 1) * LANES]


def iota(shape, dim):
    return lax.broadcasted_iota(jnp.int32, shape, dim).astype(F32)


def call(fn, outs, scratch, *args, smem=(), smem_out=(), cost=None):
    def spec(space):
        return pl.BlockSpec(memory_space=space)

    in_specs = [spec(pltpu.SMEM if i in smem else pltpu.VMEM) for i in range(len(args))]
    out_specs = [spec(pltpu.SMEM if i in smem_out else pltpu.VMEM) for i in range(len(outs))]
    return pl.pallas_call(
        fn,
        out_shape=[jax.ShapeDtypeStruct(*o) for o in outs],
        in_specs=in_specs,
        out_specs=out_specs,
        scratch_shapes=scratch,
        compiler_params=pltpu.CompilerParams(vmem_limit_bytes=VMEM_LIMIT),
        cost_estimate=cost,
    )(*args)


def pack_kernel(tok, seg, out, scr):
    count, feats, width = tok.shape
    lay(scr, tok[...].astype(F32).reshape(count * feats, width))
    row = seg[...].astype(F32)
    for f in range(feats):
        out[f, :count, :] = take(scr, f, count, feats).astype(BF)
        out[f, count:, :] = jnp.zeros((PAD, width), BF)
        out[f, count:, :count] = jnp.broadcast_to(row, (PAD, count)).astype(BF)


def codes(pos, starts):
    cls = jnp.zeros_like(pos)
    for st in starts:
        cls = cls + jnp.where(pos >= st, 1.0, 0.0)
    return jnp.where(cls >= CLASSES - 1, pos + CLASSES, cls)


def tile_range(start_ref, first, total):
    last = first + TILE - 1
    lo = jnp.int32(0)
    hi = start_ref[1]
    for c in range(1, CLASSES - 1):
        st = start_ref[c]
        lo = jnp.where(first >= st, st, lo)
        hi = jnp.where(last >= st, start_ref[c + 1], hi)
    pad = start_ref[CLASSES - 1]
    lo = jnp.where(first >= pad, first, lo)
    hi = jnp.where(last >= pad, first + TILE, hi)
    return lo // TILE, (hi + TILE - 1) // TILE


def permute_block(rank_row, first, rows, total):
    pos = iota((rows, LANES), 0) + first.astype(F32)
    parts = []
    for j in range(total // LANES):
        hit = rank_row[0:1, j * LANES : (j + 1) * LANES] == pos
        parts.append(jnp.where(hit, 1.0, 0.0).astype(BF))
    return jnp.concatenate(parts, -1)


def unpermute_block(rank_col, total):
    rows = rank_col.shape[0]
    parts = []
    for j in range(total // LANES):
        pos = iota((1, LANES), 1) + float(j * LANES)
        parts.append(jnp.where(rank_col == pos, 1.0, 0.0).astype(BF))
    return jnp.concatenate(parts, -1)


def fwd_kernel(hpd, hl, r_ref, *refs):
    xparts = refs[:hpd]
    (g1, b1, wqt, wk, wvt) = refs[hpd : hpd + 5]
    (o_send, xs_out, ot_out, lse_out, rank_row, rank_col, start_ref) = refs[hpd + 5 : hpd + 12]
    (x_scr, seg_scr, qtz, k_scr, vt, o_scr, code_col, code_row, acc, top) = refs[hpd + 12 :]
    feats = xparts[0].shape[0]
    count = xparts[0].shape[1] - PAD
    total = x_scr.shape[0]
    cl = hl * HD
    r = r_ref[0]
    chunks = total // LANES

    for s in range(hpd):
        for k in range(feats):
            at = (s * feats + k) * count
            x_scr[at : at + count, :] = xparts[s][k, :count, :]
            row = xparts[s][k, count : count + PAD, :LANES].astype(F32)[0:1]
            col = jnp.transpose(jnp.broadcast_to(row, (LANES, LANES)))
            seg_scr[at : at + count, :] = col[:count, :]

    seg = seg_scr[...]
    cls = jnp.where(seg < 0.0, float(CLASSES - 1), seg)
    seg_scr[...] = cls * 8192.0 + iota((total, LANES), 0)
    key_rows = []
    for j in range(chunks):
        blk = seg_scr[j * LANES : (j + 1) * LANES, :]
        key_rows.append(jnp.transpose(blk)[0:8, :])

    def count_less(i, carry):
        blk = seg_scr[pl.ds(pl.multiple_of(i * 64, 64), 64), :]
        out = []
        for j in range(chunks):
            less = jnp.where(blk < key_rows[j][0:1], 1.0, 0.0)
            out.append(carry[j] + jnp.sum(less.reshape(8, 8, LANES), 0))
        return tuple(out)

    ranks = lax.fori_loop(
        0, total // 64, count_less, tuple(jnp.zeros((8, LANES), F32) for _ in range(chunks))
    )
    for j in range(chunks):
        row = jnp.sum(ranks[j], 0, keepdims=True)
        rank_row[:, j * LANES : (j + 1) * LANES] = jnp.broadcast_to(row, (8, LANES))
        rank_col[j * LANES : (j + 1) * LANES, :] = jnp.transpose(
            jnp.broadcast_to(row, (LANES, LANES))
        )
    starts = []
    keys = jnp.concatenate([k[0:1] for k in key_rows], 0)
    for c in range(1, CLASSES):
        st = jnp.sum(jnp.where(keys < c * 8192.0, 1.0, 0.0))
        starts.append(st)
        start_ref[c] = st.astype(jnp.int32)
    start_ref[0] = jnp.int32(0)
    for c in range(CLASSES, 8):
        start_ref[c] = jnp.int32(total)
    code_col[...] = codes(iota((total, LANES), 0), starts)
    code_row[...] = codes(iota((8, total), 1), starts)

    qtz[...] = jnp.zeros_like(qtz)
    ones = jnp.where(iota((16, total), 0) == 0.0, 1.0, 0.0).astype(BF)
    for h in range(hl):
        vt[h, HD:, :] = ones

    def project(b, _):
        at = pl.multiple_of(b * TILE, TILE)
        block = dot(permute_block(rank_row, at, TILE, total), x_scr[...])
        xs_out[pl.ds(at, TILE), :] = block.astype(BF)
        n, _r = ln_parts(block)
        h1 = (n * g1[...] + b1[...]).astype(BF)
        qt = dot_nt(wqt[...], h1).astype(BF)
        k_scr[pl.ds(at, TILE), :] = dot(h1, wk[...]).astype(BF)
        vv = dot_nt(wvt[...], h1).astype(BF)
        for h in range(hl):
            sub = (h % 2) * HD
            qtz[h, sub : sub + HD, pl.ds(at, TILE)] = qt[h * HD : (h + 1) * HD]
            vt[h, :HD, pl.ds(at, TILE)] = vv[h * HD : (h + 1) * HD]
        return 0

    lax.fori_loop(0, total // TILE, project, 0)

    def attend(b, _):
        at = pl.multiple_of(b * TILE, TILE)
        t0, t1 = tile_range(start_ref, at, total)
        acc[...] = jnp.zeros_like(acc)
        top[...] = jnp.full_like(top, NEGATIVE)
        crow = code_row[0:1, pl.ds(at, TILE)]

        def step(t, _):
            kt = pl.multiple_of(t * TILE, TILE)
            ccol = code_col[pl.ds(kt, TILE), :]
            ccol = jnp.concatenate([ccol] * (TILE // LANES), -1)
            seen = ccol == crow
            for h in range(hl):
                pair = (h // 2) * LANES
                s = dot(k_scr[pl.ds(kt, TILE), pair : pair + LANES], qtz[h, :, pl.ds(at, TILE)])
                s = jnp.where(seen, s, NEGATIVE)
                old = top[h, 0:1, :]
                new = jnp.maximum(old, jnp.max(s, 0, keepdims=True))
                p = jnp.exp(s - new).astype(BF)
                o = dot(vt[h, :, pl.ds(kt, TILE)], p)
                acc[h] = acc[h] * jnp.exp(old - new) + o
                top[h] = jnp.broadcast_to(new, (8, TILE))
            return 0

        lax.fori_loop(t0, t1, step, 0)
        outs = []
        for h in range(hl):
            total_h = acc[h, HD : HD + 1, :]
            outs.append(acc[h, :HD, :] / total_h)
            lse_out[h : h + 1, pl.ds(at, TILE)] = top[h, 0:1, :] + jnp.log(total_h)
        ot = jnp.concatenate(outs, 0)
        ot_out[:, pl.ds(at, TILE)] = ot.astype(BF)
        o_scr[pl.ds(at, TILE), :] = jnp.transpose(ot).astype(BF)
        return 0

    lax.fori_loop(0, total // TILE, attend, 0)

    group = feats // 2
    for blk in range(total // (group * count)):
        at = blk * group * count
        hot = unpermute_block(rank_col[at : at + group * count, :], total)
        o = dot(hot, o_scr[...]).astype(BF)
        for j in range(group):
            s, k = divmod(blk * group + j, feats)
            dest = k * hpd + lax.rem(r - s + hpd, hpd)
            o_send[dest] = o[j * count : (j + 1) * count]


def prep_kernel(hl, xs, g1, b1, wqt, wq, wk, wkt, wv, k_out, kt_out, v_out, qtz, qz, h1t):
    total = xs.shape[0]
    cl = hl * HD
    qtz[...] = jnp.zeros_like(qtz)
    lane = iota((1, LANES), 1)

    def project(b, _):
        at = pl.multiple_of(b * TILE, TILE)
        n, _r = ln_parts(xs[pl.ds(at, TILE), :].astype(F32))
        h1f = n * g1[...] + b1[...]
        h1 = h1f.astype(BF)
        h1t[:, pl.ds(at, TILE)] = jnp.transpose(h1f).astype(BF)
        qt = dot_nt(wqt[...], h1).astype(BF)
        q = dot(h1, wq[...])
        k_out[pl.ds(at, TILE), :] = dot(h1, wk[...]).astype(BF)
        v_out[pl.ds(at, TILE), :] = dot(h1, wv[...]).astype(BF)
        kt_out[:, pl.ds(at, TILE)] = dot_nt(wkt[...], h1).astype(BF)
        for h in range(hl):
            sub = (h % 2) * HD
            pair = (h // 2) * LANES
            qtz[h, sub : sub + HD, pl.ds(at, TILE)] = qt[h * HD : (h + 1) * HD]
            mine = (lane >= sub) & (lane < sub + HD)
            qz[h, pl.ds(at, TILE), :] = jnp.where(mine, q[:, pair : pair + LANES], 0.0).astype(BF)
        return 0

    lax.fori_loop(0, total // TILE, project, 0)


def bwd_kernel(
    hpd,
    hl,
    r_ref,
    f_ref,
    start_ref,
    do_recv,
    xs,
    k_in,
    kt_in,
    v_in,
    qtz,
    qz,
    h1t,
    w3,
    ot,
    lse,
    rank_row,
    rank_col,
    *refs,
):
    feats = do_recv.shape[0] // hpd
    count = do_recv.shape[1]
    total = xs.shape[0]
    width = xs.shape[1]
    cl = hl * HD
    dh_outs = refs[:hpd]
    g_keep, g_send = refs[hpd : hpd + 2]
    (do_scr, dotz, doz, dots, dqt, dqkv, dh_scr, dw_scr, code_col, code_row, dv_acc, dk_acc) = refs[
        hpd + 2 :
    ]
    r = r_ref[0]
    f = f_ref[0]
    lane = iota((1, LANES), 1)

    for s in range(hpd):
        for k in range(feats):
            at = (s * feats + k) * count
            do_scr[at : at + count, :] = do_recv[k * hpd + lax.rem(r - s + hpd, hpd)]
    starts = [start_ref[c].astype(F32) for c in range(1, CLASSES)]
    code_col[...] = codes(iota((total, LANES), 0), starts)
    code_row[...] = codes(iota((8, total), 1), starts)
    dotz[...] = jnp.zeros_like(dotz)

    def arrange(b, _):
        at = pl.multiple_of(b * TILE, TILE)
        block = dot(permute_block(rank_row, at, TILE, total), do_scr[...])
        blockt = jnp.transpose(block)
        prod = blockt * ot[:, pl.ds(at, TILE)].astype(F32)
        for h in range(hl):
            sub = (h % 2) * HD
            pair = (h // 2) * LANES
            mine = (lane >= sub) & (lane < sub + HD)
            dotz[h, sub : sub + HD, pl.ds(at, TILE)] = blockt[h * HD : (h + 1) * HD].astype(BF)
            doz[h, pl.ds(at, TILE), :] = jnp.where(mine, block[:, pair : pair + LANES], 0.0).astype(BF)
            dots[h : h + 1, pl.ds(at, TILE)] = jnp.sum(prod[h * HD : (h + 1) * HD], 0, keepdims=True)
        return 0

    lax.fori_loop(0, total // TILE, arrange, 0)
    dqt[...] = jnp.zeros_like(dqt)

    def keys(b, _):
        kt = pl.multiple_of(b * TILE, TILE)
        t0, t1 = tile_range(start_ref, kt, total)
        ccol = code_col[pl.ds(kt, TILE), :]
        ccol = jnp.concatenate([ccol] * (TILE // LANES), -1)
        dv_acc[...] = jnp.zeros_like(dv_acc)
        dk_acc[...] = jnp.zeros_like(dk_acc)

        def step(t, _):
            at = pl.multiple_of(t * TILE, TILE)
            seen = ccol == code_row[0:1, pl.ds(at, TILE)]
            for h in range(hl):
                pair = (h // 2) * LANES
                kb = k_in[pl.ds(kt, TILE), pair : pair + LANES]
                vb = v_in[pl.ds(kt, TILE), pair : pair + LANES]
                s = dot(kb, qtz[h, :, pl.ds(at, TILE)])
                p = jnp.where(seen, jnp.exp(s - lse[h : h + 1, pl.ds(at, TILE)]), 0.0)
                dp = dot(vb, dotz[h, :, pl.ds(at, TILE)])
                ds = (p * (dp - dots[h : h + 1, pl.ds(at, TILE)])).astype(BF)
                dv_acc[h // 2] += dot(p.astype(BF), doz[h, pl.ds(at, TILE), :])
                dk_acc[h // 2] += dot(ds, qz[h, pl.ds(at, TILE), :])
                rows = slice(h * HD, (h + 1) * HD)
                dqt[rows, pl.ds(at, TILE)] += dot(kt_in[rows, pl.ds(kt, TILE)], ds)
            return 0

        lax.fori_loop(t0, t1, step, 0)
        for p2 in range((hl + 1) // 2):
            lo = p2 * LANES
            dqkv[pl.ds(kt, TILE), cl + lo : cl + lo + LANES] = dk_acc[p2].astype(BF)
            dqkv[pl.ds(kt, TILE), 2 * cl + lo : 2 * cl + lo + LANES] = dv_acc[p2].astype(BF)
        return 0

    lax.fori_loop(0, total // TILE, keys, 0)

    def finish(b, carry):
        at = pl.multiple_of(b * TILE, TILE)
        dq = jnp.transpose(dqt[:, pl.ds(at, TILE)]) * SCALING
        dqkv[pl.ds(at, TILE), :cl] = dq.astype(BF)
        dh = dot_nt(dqkv[pl.ds(at, TILE), :], w3[...])
        n, _r = ln_parts(xs[pl.ds(at, TILE), :].astype(F32))
        dh_scr[pl.ds(at, TILE), :] = dh.astype(BF)
        return (
            carry[0] + jnp.sum((dh * n).reshape(TILE // 8, 8, width), 0),
            carry[1] + jnp.sum(dh.reshape(TILE // 8, 8, width), 0),
        )

    zero = jnp.zeros((8, width), F32)
    gg, gb = lax.fori_loop(0, total // TILE, finish, (zero, zero))

    for c in range(3):
        dw_scr[:, c * cl : (c + 1) * cl] = dot(h1t[...], dqkv[:, c * cl : (c + 1) * cl]).astype(BF)
    rows = width // feats
    extra = jnp.concatenate([jnp.sum(gg, 0, keepdims=True), jnp.sum(gb, 0, keepdims=True)], 0)
    extra = jnp.concatenate([extra, jnp.zeros((6, width), F32)], 0).astype(BF)
    half = feats // 2
    for e in range(feats):
        ref, at = (g_keep, e) if e < half else (g_send, e - half)
        src = pl.multiple_of(lax.bitwise_xor(f, e) * rows, rows)
        ref[at, :rows, :] = dw_scr[pl.ds(src, rows), :]
        for c in range(0, width, cl):
            ref[at, rows + 8 * (c // cl) : rows + 8 * (c // cl) + 8, :cl] = extra[:, c : c + cl]
        for c in range(0, width, cl):
            ref[at, rows + 8 * (c // cl) : rows + 8 * (c // cl) + 8, cl:] = jnp.zeros((8, 2 * cl), BF)

    group = feats // 2
    for blk in range(total // (group * count)):
        at = blk * group * count
        hot = unpermute_block(rank_col[at : at + group * count, :], total)
        o = dot(hot, dh_scr[...]).astype(BF)
        for j in range(group):
            s, k = divmod(blk * group + j, feats)
            dh_outs[s][k] = o[j * count : (j + 1) * count]


def norm_kernel(hpd, *refs):
    parts = refs[:hpd]
    x, g1, out = refs[hpd:]
    feats, count, _w = parts[0].shape
    for k in range(feats):
        dh = parts[0][k].astype(F32)
        for s in range(1, hpd):
            dh = dh + parts[s][k].astype(F32)
        n, r = ln_parts(x[k, :count, :].astype(F32))
        out[k] = ln_back(dh, n, r, g1[...]).astype(BF)


def final_kernel(dx1, dv, out, scr):
    feats, count, width = dv.shape
    for f in range(feats):
        val = dx1[f * count : (f + 1) * count, :] + dv[f].astype(F32)
        place(scr, f, count, feats, val)
    out[...] = lift(scr).reshape(count, feats, width)


def rows_kernel(
    hpd,
    order,
    me_ref,
    o_recv,
    xt,
    cot,
    g2,
    b2,
    g3,
    b3,
    ub,
    db,
    wso,
    wfq,
    wfo,
    wup,
    wdn,
    out,
    dx1,
    do_send,
    g_keep,
    g_send,
    wide,
    ct,
    o1,
    x1,
    h2,
    qkv,
    o2,
    x2,
    h3,
    u,
    dz,
    dx2,
    do2,
    dqkv,
    pscr,
    tr,
    wblk,
    ubg,
    wdn_scr,
):
    feats = xt.shape[0]
    count = xt.shape[1] - PAD
    width = xt.shape[2]
    rows = feats * count
    hidden = wup.shape[1]
    n = o_recv.shape[0]
    cl = o_recv.shape[2]
    half = rows // 2
    me = me_ref[0]
    lane = iota((1, LANES), 1)
    part = 16
    tiles = count // part
    size = feats * part

    lay(wide, cot[...].astype(F32).reshape(rows, width))
    for f in range(feats):
        ct[f * count : (f + 1) * count, :] = take(wide, f, count, feats).astype(BF)
        for c in range(hpd):
            o1[f * count : (f + 1) * count, c * cl : (c + 1) * cl] = o_recv[f * hpd + c]

    for b in range(2):
        at = slice(b * half, (b + 1) * half)
        x = xt[b * feats // 2 : (b + 1) * feats // 2, :count, :].astype(F32).reshape(half, width)
        v = x + dot(o1[at, :], wso[...])
        x1[at, :] = v
        nn, _r = ln_parts(v)
        h2[at, :] = (nn * g2[...] + b2[...]).astype(BF)

    qkv3 = qkv

    def qkv_step(c, _):
        cols = pl.ds(pl.multiple_of(c * TILE, TILE), TILE)
        scale = jnp.where(c < width // TILE, SCALING, 1.0)
        y = dot(h2[...], wfq[:, cols])
        qkv3[:, :, cols] = (y * scale).astype(BF).reshape(feats, count, TILE)
        return 0

    lax.fori_loop(0, 3 * width // TILE, qkv_step, 0)

    ri = lax.broadcasted_iota(jnp.int32, (size, size), 0)
    ci = lax.broadcasted_iota(jnp.int32, (size, size), 1)
    same = lax.rem(ri, part) == lax.rem(ci, part)

    def masked(v, h):
        sub = (h % 2) * HD
        return jnp.where((lane >= sub) & (lane < sub + HD), v, 0.0).astype(BF)

    def feat_fwd(t, _):
        at = pl.ds(pl.multiple_of(t * part, part), part)
        for p2 in range(H // 2):
            lo = p2 * LANES
            q = qkv3[:, at, lo : lo + LANES].reshape(size, LANES)
            k = qkv3[:, at, width + lo : width + lo + LANES].reshape(size, LANES)
            v = qkv3[:, at, 2 * width + lo : 2 * width + lo + LANES].reshape(size, LANES)
            o = jnp.zeros((size, LANES), F32)
            for h in (2 * p2, 2 * p2 + 1):
                s = dot_nt(q, masked(k, h))
                s = jnp.where(same, s, NEGATIVE)
                e = jnp.exp(s - jnp.max(s, -1, keepdims=True))
                p = (e / jnp.sum(e, -1, keepdims=True)).astype(BF)
                pscr[t, h] = p
                o = o + dot(p, masked(v, h))
            o2[:, at, lo : lo + LANES] = o.astype(BF).reshape(feats, part, LANES)
        return 0

    lax.fori_loop(0, tiles, feat_fwd, 0)

    for b in range(2):
        at = slice(b * half, (b + 1) * half)
        o = o2[b * feats // 2 : (b + 1) * feats // 2, :, :].reshape(half, width)
        v = x1[at, :] + dot(o, wfo[...])
        x2[at, :] = v
        nn, _r = ln_parts(v)
        h3[at, :] = (nn * g3[...] + b3[...]).astype(BF)

    def ffn(c, _):
        cols = pl.ds(pl.multiple_of(c * TILE, TILE), TILE)
        total = jnp.zeros((8, TILE), F32)
        for b in range(2):
            at = slice(b * half, (b + 1) * half)
            z = dot(h3[at, :], wup[:, cols]) + ub[0:1, cols]
            zz = z * z
            th = jnp.tanh(GELU_C * z * (1.0 + GELU_A * zz))
            h1p = 0.5 * (1.0 + th)
            u[at, cols] = (z * h1p).astype(BF)
            slope = h1p + 0.5 * z * (1.0 - th * th) * (GELU_C * (1.0 + 3.0 * GELU_A * zz))
            du = dot_nt(ct[at, :], wdn[cols, :])
            d = (du * slope).astype(BF)
            dz[at, cols] = d
            total = total + jnp.sum(d.astype(F32).reshape(half // 8, 8, TILE), 0)
        ubg[:, cols] = total
        return 0

    lax.fori_loop(0, hidden // TILE, ffn, 0)

    vectors = []
    gg = jnp.zeros((1, width), F32)
    gb = jnp.zeros((1, width), F32)
    gd = jnp.zeros((1, width), F32)
    for b in range(2):
        at = slice(b * half, (b + 1) * half)
        y = x2[at, :] + dot(u[at, :], wdn[...]) + db[...]
        for j in range(feats // 2):
            f = b * (feats // 2) + j
            place(wide, f, count, feats, y[j * count : (j + 1) * count])
        dh = dot_nt(dz[at, :], wup[...])
        nn, r = ln_parts(x2[at, :])
        c = ct[at, :].astype(F32)
        gg = gg + jnp.sum(dh * nn, 0, keepdims=True)
        gb = gb + jnp.sum(dh, 0, keepdims=True)
        gd = gd + jnp.sum(c, 0, keepdims=True)
        v = c + ln_back(dh, nn, r, g3[...])
        dx2[at, :] = v
        do2[b * feats // 2 : (b + 1) * feats // 2, :, :] = (
            dot_nt(v.astype(BF), wfo[...]).astype(BF).reshape(feats // 2, count, width)
        )
    out[...] = lift(wide).reshape(count, feats, width).astype(BF)
    vectors = [gg, gb, gd]

    def feat_bwd(t, _):
        at = pl.ds(pl.multiple_of(t * part, part), part)
        for p2 in range(H // 2):
            lo = p2 * LANES
            q = qkv3[:, at, lo : lo + LANES].reshape(size, LANES)
            k = qkv3[:, at, width + lo : width + lo + LANES].reshape(size, LANES)
            v = qkv3[:, at, 2 * width + lo : 2 * width + lo + LANES].reshape(size, LANES)
            g = do2[:, at, lo : lo + LANES].reshape(size, LANES)
            dq = jnp.zeros((size, LANES), F32)
            dk = jnp.zeros((size, LANES), F32)
            dv = jnp.zeros((size, LANES), F32)
            for h in (2 * p2, 2 * p2 + 1):
                p = pscr[t, h]
                pf = p.astype(F32)
                dp = dot_nt(g, masked(v, h))
                ds = pf * (dp - jnp.sum(pf * dp, -1, keepdims=True))
                dst = jnp.transpose(ds).astype(BF)
                pt = jnp.transpose(pf).astype(BF)
                dq = dq + dot(ds.astype(BF), masked(k, h))
                dk = dk + dot(dst, masked(q, h))
                dv = dv + dot(pt, masked(g, h))
            dqkv[:, at, lo : lo + LANES] = (dq * SCALING).astype(BF).reshape(feats, part, LANES)
            dqkv[:, at, width + lo : width + lo + LANES] = dk.astype(BF).reshape(feats, part, LANES)
            dqkv[:, at, 2 * width + lo : 2 * width + lo + LANES] = dv.astype(BF).reshape(
                feats, part, LANES
            )
        return 0

    lax.fori_loop(0, tiles, feat_bwd, 0)

    gg = jnp.zeros((1, width), F32)
    gb = jnp.zeros((1, width), F32)
    for b in range(2):
        at = slice(b * half, (b + 1) * half)
        d = dqkv[b * feats // 2 : (b + 1) * feats // 2, :, :].reshape(half, 3 * width)
        dh = dot_nt(d, wfq[...])
        nn, r = ln_parts(x1[at, :])
        gg = gg + jnp.sum(dh * nn, 0, keepdims=True)
        gb = gb + jnp.sum(dh, 0, keepdims=True)
        v = dx2[at, :] + ln_back(dh, nn, r, g2[...])
        dx1[at, :] = v
        g = dot_nt(v.astype(BF), wso[...]).astype(BF)
        for j in range(feats // 2):
            f = b * (feats // 2) + j
            for c in range(hpd):
                do_send[f * hpd + c] = g[j * count : (j + 1) * count, c * cl : (c + 1) * cl]
    vectors = [gg, gb] + vectors

    bits = len(order)

    def slot(pos):
        rel = 0
        for i, bit in enumerate(order):
            if (pos >> (bits - 1 - i)) & 1:
                rel |= 1 << bit
        ref, at = (g_keep, pos) if pos < n // 2 else (g_send, pos - n // 2)
        return ref, at, lax.bitwise_xor(me, rel)

    piece = width // n
    fpiece = hidden // n

    def spread(base):
        for pos in range(n):
            ref, at, d = slot(pos)
            src = pl.multiple_of(d * piece, piece)
            ref[at, base : base + piece, :] = wblk[pl.ds(src, piece), :]

    base = 0
    for b in range(hidden // width):
        tr[...] = flip(u[:, b * width : (b + 1) * width])
        wdn_scr[b * width : (b + 1) * width, :] = dot(tr[...], ct[...]).astype(BF)
    for pos in range(n):
        ref, at, d = slot(pos)
        src = pl.multiple_of(d * fpiece, fpiece)
        ref[at, base : base + fpiece, :] = wdn_scr[pl.ds(src, fpiece), :]
    base += fpiece
    tr[...] = flip(h3[...])
    for b in range(hidden // width):
        wblk[...] = dot(tr[...], dz[:, b * width : (b + 1) * width]).astype(BF)
        spread(base)
        base += piece
    tr[...] = flip(h2[...])
    for b in range(3):
        d = dqkv[:, :, b * width : (b + 1) * width].reshape(rows, width)
        wblk[...] = dot(tr[...], d).astype(BF)
        spread(base)
        base += piece
    tr[...] = flip(o2[...].reshape(rows, width))
    wblk[...] = dot(tr[...], dx2[...].astype(BF)).astype(BF)
    spread(base)
    base += piece
    tr[...] = flip(o1[...])
    wblk[...] = dot(tr[...], dx1[...].astype(BF)).astype(BF)
    spread(base)
    base += piece
    ubs = jnp.sum(ubg[...], 0, keepdims=True)
    vectors = vectors + [ubs[:, b * width : (b + 1) * width] for b in range(hidden // width)]
    vec = jnp.concatenate(vectors + [jnp.zeros((16 - len(vectors), width), F32)], 0).astype(BF)
    for pos in range(n):
        ref, at, _d = slot(pos)
        ref[at, base : base + 16, :] = vec


def solution(mesh):
    n = mesh.shape["samp"]
    groups = mesh.shape["grp"]
    bits = n.bit_length() - 1
    order = [b for b in (0, 1) if b < bits] + list(range(bits - 1, 1, -1))

    def flip_perm(bit):
        return [(d, d ^ (1 << bit)) for d in range(n)]

    def add(a, b):
        return (a.astype(F32) + b.astype(F32)).astype(BF)

    def halve(keep, send, perms):
        for i, perm in enumerate(perms):
            got = lax.ppermute(send, "samp", perm)
            both = add(keep, got)
            if i + 1 < len(perms):
                h = both.shape[0] // 2
                keep, send = both[:h], both[h:]
        return both

    def across(v):
        step = 1
        while step < groups:
            got = lax.ppermute(v, "grp", [(d, d ^ step) for d in range(groups)])
            v = add(v, got)
            step *= 2
        return v

    def body(
        tokens,
        segments,
        cotangent,
        first_gain,
        first_shift,
        sample_qkv,
        sample_out,
        second_gain,
        second_shift,
        feature_qkv,
        feature_out,
        third_gain,
        third_shift,
        up_weight,
        up_bias,
        down_weight,
        down_bias,
    ):
        count, feats, width = tokens.shape[1:]
        hidden = up_weight.shape[1]
        rows = count * feats
        hpd = n // feats
        hl = H // hpd
        cl = hl * HD
        total = n * count
        heads8 = 8
        me = lax.axis_index("samp")
        r = lax.rem(me, hpd)
        f = me // hpd
        r1, f1, me1 = (v.reshape(1).astype(jnp.int32) for v in (r, f, me))
        peers = [[q + hpd * k for k in range(feats)] for q in range(hpd)]
        g1, b1, g2, b2, g3, b3, ub, db = (
            v.reshape(1, -1)
            for v in (
                first_gain,
                first_shift,
                second_gain,
                second_shift,
                third_gain,
                third_shift,
                up_bias,
                down_bias,
            )
        )

        def shift(s):
            return [(d, d // hpd * hpd + (d % hpd + s) % hpd) for d in range(n)]

        (xt,) = call(
            pack_kernel,
            [((feats, count + PAD, width), BF)],
            [pltpu.VMEM((width // LANES, rows, LANES), F32)],
            tokens[0],
            segments,
        )
        mine = lax.all_to_all(xt, "samp", 0, 0, tiled=True, axis_index_groups=peers)
        xparts = [mine] + [lax.ppermute(mine, "samp", shift(s)) for s in range(1, hpd)]

        def columns(c):
            return lax.dynamic_slice_in_dim(sample_qkv, c * width + r * cl, cl, 1)

        wq = columns(0) * BF(SCALING)
        wk = columns(1)
        wv = columns(2)
        w3 = jnp.concatenate([columns(0), wk, wv], 1)

        o_send, xs, ot, lse, rank_row, rank_col, starts = call(
            functools.partial(fwd_kernel, hpd, hl),
            [
                ((n, count, cl), BF),
                ((total, width), BF),
                ((cl, total), BF),
                ((heads8, total), F32),
                ((8, total), F32),
                ((total, LANES), F32),
                ((8,), jnp.int32),
            ],
            [
                pltpu.VMEM((total, width), BF),
                pltpu.VMEM((total, LANES), F32),
                pltpu.VMEM((hl, LANES, total), BF),
                pltpu.VMEM((total, cl), BF),
                pltpu.VMEM((hl, HD + 16, total), BF),
                pltpu.VMEM((total, cl), BF),
                pltpu.VMEM((total, LANES), F32),
                pltpu.VMEM((8, total), F32),
                pltpu.VMEM((hl, HD + 16, TILE), F32),
                pltpu.VMEM((hl, 8, TILE), F32),
            ],
            r1,
            *xparts,
            g1,
            b1,
            wq.T,
            wk,
            wv.T,
            smem=(0,),
            smem_out=(6,),
        )
        o_recv = lax.all_to_all(o_send, "samp", 0, 0, tiled=True)

        pieces = hidden // n + width // n * (hidden // width + 5) + 16
        vm = pltpu.VMEM
        out, dx1, do_send, g_keep, g_send = call(
            functools.partial(rows_kernel, hpd, order),
            [
                ((count, feats, width), BF),
                ((rows, width), F32),
                ((n, count, cl), BF),
                ((n // 2, pieces, width), BF),
                ((n // 2, pieces, width), BF),
            ],
            [
                vm((width // LANES, rows, LANES), F32),
                vm((rows, width), BF),
                vm((rows, width), BF),
                vm((rows, width), F32),
                vm((rows, width), BF),
                vm((feats, count, 3 * width), BF),
                vm((feats, count, width), BF),
                vm((rows, width), F32),
                vm((rows, width), BF),
                vm((rows, hidden), BF),
                vm((rows, hidden), BF),
                vm((rows, width), F32),
                vm((feats, count, width), BF),
                vm((feats, count, 3 * width), BF),
                vm((count // 16, H, 16 * feats, 16 * feats), BF),
                vm((width, rows), BF),
                vm((width, width), BF),
                vm((8, hidden), F32),
                vm((hidden, width), BF),
            ],
            me1,
            o_recv,
            xt,
            cotangent[0],
            g2,
            b2,
            g3,
            b3,
            ub,
            db,
            sample_out,
            feature_qkv,
            feature_out,
            up_weight,
            down_weight,
            smem=(0,),
        )
        do_recv = lax.all_to_all(do_send, "samp", 0, 0, tiled=True)
        upper = across(halve(g_keep, g_send, [flip_perm(b) for b in order])[0])

        k_all, kt_all, v_all, qtz, qz, h1t = call(
            functools.partial(prep_kernel, hl),
            [
                ((total, cl), BF),
                ((cl, total), BF),
                ((total, cl), BF),
                ((hl, LANES, total), BF),
                ((hl, total, LANES), BF),
                ((width, total), BF),
            ],
            [],
            xs,
            g1,
            b1,
            wq.T,
            wq,
            wk,
            wk.T,
            wv,
        )
        extra = 8 * (width // cl)
        res = call(
            functools.partial(bwd_kernel, hpd, hl),
            [((feats, count, width), BF)] * hpd
            + [((feats // 2, width // feats + extra, 3 * cl), BF)] * 2,
            [
                vm((total, cl), BF),
                vm((hl, LANES, total), BF),
                vm((hl, total, LANES), BF),
                vm((8, total), F32),
                vm((cl, total), F32),
                vm((total, 3 * cl), BF),
                vm((total, width), BF),
                vm((width, 3 * cl), BF),
                vm((total, LANES), F32),
                vm((8, total), F32),
                vm(((hl + 1) // 2, TILE, LANES), F32),
                vm(((hl + 1) // 2, TILE, LANES), F32),
            ],
            r1,
            f1,
            starts,
            do_recv,
            xs,
            k_all,
            kt_all,
            v_all,
            qtz,
            qz,
            h1t,
            w3,
            ot,
            lse,
            rank_row,
            rank_col,
            smem=(0, 1, 2),
        )
        dhs, (q_keep, q_send) = res[:hpd], res[hpd:]
        parts = [dhs[0]] + [lax.ppermute(dhs[s], "samp", shift(-s)) for s in range(1, hpd)]
        (dv,) = call(
            functools.partial(norm_kernel, hpd),
            [((feats, count, width), BF)],
            [],
            *parts,
            mine,
            g1,
        )
        dv = lax.all_to_all(dv, "samp", 0, 0, tiled=True, axis_index_groups=peers)
        (grad_tokens,) = call(
            final_kernel,
            [((count, feats, width), F32)],
            [vm((width // LANES, rows, LANES), F32)],
            dx1,
            dv,
        )

        step0 = hpd.bit_length() - 1
        lower = across(halve(q_keep, q_send, [flip_perm(b) for b in range(bits - 1, step0 - 1, -1)])[0])
        piece = width // n
        main = lower[: width // feats].reshape(hpd, piece, 3, cl)
        tail = lower[width // feats :]
        vecs = [tail[8 * c : 8 * c + 8, :cl] for c in range(width // cl)]
        vec = jnp.concatenate(vecs, 1)
        cols = jnp.zeros((piece, 3, hpd, cl), BF)
        for s in range(hpd):
            give = lax.dynamic_index_in_dim(main, lax.rem(r + s, hpd), 0, keepdims=False)
            if s:
                give = lax.ppermute(give, "samp", shift(s))
            src = lax.rem(r - s + hpd, hpd)
            cols = lax.dynamic_update_slice(cols, give[:, :, None], (0, 0, src, 0))
        grad_sample_qkv = cols.reshape(piece, 3 * width).astype(F32)
        vec_sum = vec.astype(F32)
        for s in range(1, hpd):
            vec_sum = vec_sum + lax.ppermute(vec, "samp", shift(s)).astype(F32)

        def own(v):
            return lax.dynamic_slice_in_dim(v, me * (v.shape[0] // n), v.shape[0] // n, 0)

        fpiece = hidden // n
        base = fpiece
        up32 = upper.astype(F32)
        grad_down = up32[:fpiece]

        def blocks(m):
            nonlocal base
            got = [up32[base + i * piece : base + (i + 1) * piece] for i in range(m)]
            base += m * piece
            return jnp.concatenate(got, 1)

        grad_up = blocks(hidden // width)
        grad_fqkv = blocks(3)
        grad_fout = blocks(1)
        grad_sout = blocks(1)
        vu = up32[base:]
        return (
            out[None],
            grad_tokens[None],
            own(vec_sum[0]),
            own(vec_sum[1]),
            grad_sample_qkv,
            grad_sout,
            own(vu[0]),
            own(vu[1]),
            grad_fqkv,
            grad_fout,
            own(vu[2]),
            own(vu[3]),
            grad_up,
            own(vu[5 : 5 + hidden // width].reshape(-1)),
            grad_down,
            own(vu[4]),
        )

    rep = P()
    data = P("grp", "samp", None, None)
    line = P("samp")
    flat = P("samp", None)
    in_specs = (data, P("grp", "samp"), data) + (rep,) * 14
    out_specs = (
        data,
        data,
        line,
        line,
        flat,
        flat,
        line,
        line,
        flat,
        flat,
        line,
        line,
        flat,
        line,
        flat,
        line,
    )
    return jax.shard_map(body, mesh=mesh, in_specs=in_specs, out_specs=out_specs, check_vma=False)
```

time: 1050 us -> 316 us (0.30)
  matrix products: 246 us -> 0 us
  blocking collectives: 272 us -> 54 us
  waiting for transfers between devices: 254 us -> 72.7 us
  local copies, waits for them, and re-layouts: 181 us -> 21.9 us
  Pallas kernels: 0 us -> 130 us
  other arithmetic: 69.2 us -> 16.3 us
  starting transfers between devices: 0.49 us -> 19.1 us
  between operations: 17.6 us -> 0.9 us
    dot_general x31 -> x0, matrix products: 246 us -> none  [the longest x18 62.1 us: matmul(): return jnp.dot(left, right, preferred_element_type=jnp.float32)]
    all_gather x2 -> x0, blocking collectives: 174 us -> none  [the longest x1 102 us: body(): lax.all_gather(row_dots, 'samp', axis=2, tiled=True)]
    all_gather x4 -> x0, waiting for transfers between devices: 147 us -> none  [the longest x1 84.4 us: body(): lax.all_gather(key_one, 'samp', axis=0, tiled=True)]
    pallas_call x0 -> x7, Pallas kernels: none -> 130 us  [call(): pl.pallas_call(fn, out_shape=[jax.ShapeDtypeStruct(*o) for o in outs], in...]
    unnamed x2 -> x0, blocking collectives: 97.8 us -> none
    all_gather x6 -> x0, local copies, waits for them, and re-layouts: 96.9 us -> none  [the longest x1 27.2 us: body(): lax.all_gather(mixed_grad_one, 'samp', axis=0, tiled=True)]
    ppermute x0 -> x13, waiting for transfers between devices: none -> 72.7 us  [the longest x7 70.8 us: halve(): got = lax.ppermute(send, 'samp', perm)]
    reduce_scatter x6 -> x0, waiting for transfers between devices: 66.1 us -> none  [the longest x1 63 us: body(): lax.psum_scatter(grad_sample_qkv.astype(jnp.bfloat16), 'samp', scatter_di...]
  transfers between devices with their start and end apart: 12 -> 15, of which waited for: 6 -> 7; matrix products, arithmetic and copies ran while one was open for 46% -> 9% of each run, Pallas kernels for 0% -> 15%
where the time goes in v1:
time: 316 us; the launch traced here: 315 us
  Pallas kernels  130 us (41%)
  waiting for transfers between devices  72.7 us (23%)
  blocking collectives  54 us (17%)
  local copies, waits for them, and re-layouts  21.9 us (7%)
  starting transfers between devices  19.1 us (6%)
  other arithmetic  16.3 us (5%)
    pallas_call x7, Pallas kernels, call(): pl.pallas_call(fn, out_shape=[jax.ShapeDtypeStruct(*o) for o in outs], in...  130 us
    ppermute x7, waiting for transfers between devices, halve(): got = lax.ppermute(send, 'samp', perm)  70.8 us
    all_to_all x1, blocking collectives, body(): mine = lax.all_to_all(xt, 'samp', 0, 0, tiled=True, axis_index_groups=peers)  29.5 us
    all_to_all x1, blocking collectives, body(): o_recv = lax.all_to_all(o_send, 'samp', 0, 0, tiled=True)  24.5 us
    convert_element_type x6, other arithmetic, add(): return (a.astype(F32) + b.astype(F32)).astype(BF)  9.66 us
    ppermute x7, starting transfers between devices, halve(): got = lax.ppermute(send, 'samp', perm)  6.96 us
  transfers between devices with their start and end apart: 15, of which 7 were waited for; matrix products, arithmetic and copies ran while one was open for 9% of the time, Pallas kernels for 15%

profile of v1, /device:TPU:0, one launch (start us, length us, event | category | flops | bytes accessed | tf_op | source)
XLA Modules:
  0.0 315.0 jit_solution(15997416249036515062)
XLA Ops:
  0.6 2.5 shard_map.288.xt
  3.1 29.5 %all_to_all.20.refs_0_.refs_2_ = bf16[8,104,512]{2,1,0:T(8,128)(2,1)S(1)} all-to-all(bf16[8,104,512]{2,1,0:T(8,128)(2,1)} %shard_map.288.xt), channel_id=1, replica_groups={{0,2,4,6,8,10,12,14},{1,3,5,7,9,11,13,15},{16,18,20,22,24,26,28,30},{17..., dimensions={0} | all-to-all | bytes 1703936 | tf_op jit(solution)/shard_map/all_to_all | solution.py:804
  32.6 2.3 broadcast_multiply_fusion
  38.3 31.6 %shard_map.289 = (bf16[16,96,256]{2,1,0:T(8,128)(2,1)}, bf16[1536,512]{1,0:T(8,128)(2,1)}, bf16[256,1536]{1,0:T(8,128)(2,1)}, f32[8,1536]{1,0:T(8,128)}, f32[8,1...) custom-call(s32[1]{0:T(128)} %bitcast.1.r_ref, bf16[8,104,512]{2,1,0:T(8,128)(2,1)} %copy-done, ...), custom_call_target="tpu_custom_call" | custom-call | tf_op jit(solution)/shard_map/pallas_call | solution.py:84
  69.9 24.5 %all_to_all.21.o_recv = bf16[16,96,256]{2,1,0:T(8,128)(2,1)} all-to-all(bf16[16,96,256]{2,1,0:T(8,128)(2,1)} %get-tuple-element.38), channel_id=1, replica_groups=mesh['grp'=2,'samp'=16] {'samp'}, dimensions={0} | all-to-all | bytes 1572864 | tf_op jit(solution)/shard_map/all_to_all | solution.py:848
  94.4 49.5 %shard_map.290 = (bf16[96,8,512]{2,1,0:T(8,128)(2,1)}, f32[768,512]{1,0:T(8,128)}, bf16[16,96,256]{2,1,0:T(8,128)(2,1)}, bf16[8,432,512]{2,1,0:T(8,128)(2,1)}, bf16[8,432,512]{2,1,0:T(8,128)(2,1)}) custom-call(s32[1]{0:T(128)} %bitcast.me_ref, bf16[16,96,256]{2,1,0:T(8,128)(2,1)} %all_to_all.21.o_recv, bf16[8,104,512]{2,1,0:T(8,128)(2,1)} %shard_map.288.xt, ...), custom_call_target="tpu_custom_call" | custom-call | tf_op jit(solution)/shard_map/pallas_call | solution.py:84
  144.7 4.5 %all-to-all-start.2 = ((bf16[16,96,256]{2,1,0:T(8,128)(2,1)}), bf16[16,96,256]{2,1,0:T(8,128)(2,1)}, u32[]{:S(2)}, u32[]{:S(2)}) async-start(bf16[16,96,256]{2,1,0:T(8,128)(2,1)} %get-tuple-element.42), calls=%async_computation.2 | async-start | bytes 1572864 | tf_op jit(solution)/shard_map/all_to_all | solution.py:899
  152.5 4.1 %add_convert_fusion = bf16[8,432,512]{2,1,0:T(8,128)(2,1)S(1)} fusion(bf16[8,432,512]{2,1,0:T(8,128)(2,1)} %copy-done.4, bf16[8,432,512]{2,1,0:T(8,128)(2,1)} %get-tuple-element.58), kind=kLoop, calls=%fused_computation | loop fusion | flops 7077888 | bytes 10616832 | tf_op jit(solution)/shard_map/convert_element_type | solution.py:729
  160.5 2.0 pad_maximum_fusion.w3
  162.5 9.0 %shard_map.291 = (bf16[1536,256]{1,0:T(8,128)(2,1)}, bf16[256,1536]{1,0:T(8,128)(2,1)}, bf16[1536,256]{1,0:T(8,128)(2,1)}, bf16[4,128,1536]{2,1,0:T(8,128)(2,1)}...) custom-call(bf16[1536,512]{1,0:T(8,128)(2,1)} %get-tuple-element.43.xs, f32[1,512]{1,0:T(1,128)} %bitcast.54, ...), custom_call_target="tpu_custom_call" | custom-call | tf_op jit(solution)/shard_map/pallas_call | solution.py:84
  171.6 30.6 %shard_map.292 = (bf16[8,96,512]{2,1,0:T(8,128)(2,1)}, bf16[8,96,512]{2,1,0:T(8,128)(2,1)}, bf16[4,80,768]{2,1,0:T(8,128)(2,1)}, bf16[4,80,768]{2,1,0:T(8,128)(2,1)}) custom-call(s32[1]{0:T(128)} %bitcast.1.r_ref, s32[1]{0:T(128)} %bitcast.15.f_ref, s32[8]{0:T(128)} %get-tuple-element.41.start_ref, bf16[16,96,256]{2,1,0:T(8,128)(2,1)} %all-to-all-done.2.do_recv, ...), custom_call_target="tpu_custom_call" | custom-call | tf_op jit(solution)/shard_map/pallas_call | solution.py:84
  203.8 23.3 %collective-permute-done.2 = bf16[4,80,768]{2,1,0:T(8,128)(2,1)S(1)} collective-permute-done((bf16[4,80,768]{2,1,0:T(8,128)(2,1)}, bf16[4,80,768]{2,1,0:T(8,128)(2,1)S(1)}, u32[]{:S(2)}, u32[]{:S(2)}) %collective-permute-start.2) | collective-permute-done | bytes 491552 | tf_op jit(solution)/shard_map/ppermute | solution.py:733
  228.3 2.0 add_convert_fusion.1
  231.6 2.9 collective-permute-start.10
  234.4 3.0 collective-permute-done.3
  238.3 4.2 %collective-permute-done.4 = bf16[1,80,768]{2,1,0:T(8,128)(2,1)S(1)} collective-permute-done((bf16[1,80,768]{2,1,0:T(8,128)(2,1)S(1)}, bf16[1,80,768]{2,1,0:T(8,128)(2,1)S(1)}, u32[]{:S(2)}, u32[]{:S(2)}) %collective-permute-start.4) | collective-permute-done | bytes 122912 | tf_op jit(solution)/shard_map/ppermute | solution.py:733
  244.7 3.6 %shard_map.293 = bf16[8,96,512]{2,1,0:T(8,128)(2,1)} custom-call(bf16[8,96,512]{2,1,0:T(8,128)(2,1)} %get-tuple-element.54.refs_0_, bf16[8,96,512]{2,1,0:T(8,128)(2,1)} %collective-permute-done.1.refs_1_, bf16[8,104,512]{2,1,0:T(8,128)(2,1)} %copy-done, f32[1,512]{1,0:T(1,128)} %bitcast.55), custom_call_target="tpu_custom_call" | custom-call | tf_op jit(solution)/shard_map/pallas_call | solution.py:84
  248.3 4.0 %all-to-all-start.3 = ((bf16[8,96,512]{2,1,0:T(8,128)(2,1)}), bf16[8,96,512]{2,1,0:T(8,128)(2,1)S(1)}, u32[]{:S(2)}, u32[]{:S(2)}) async-start(bf16[8,96,512]{2,1,0:T(8,128)(2,1)} %shard_map.293), calls=%async_computation.3 | async-start | bytes 1572864 | tf_op jit(solution)/shard_map/all_to_all | solution.py:969
  254.6 27.9 %collective-permute-done.10 = bf16[2,432,512]{2,1,0:T(8,128)(2,1)} collective-permute-done((bf16[2,432,512]{2,1,0:T(8,128)(2,1)S(1)}, bf16[2,432,512]{2,1,0:T(8,128)(2,1)}, u32[]{:S(2)}, u32[]{:S(2)}) %collective-permute-start.10) | collective-permute-done | bytes 884768 | tf_op jit(solution)/shard_map/ppermute | solution.py:733
  285.6 2.0 dynamic_update_slice.6
  287.6 10.8 %collective-permute-done.11 = bf16[1,432,512]{2,1,0:T(8,128)(2,1)S(1)} collective-permute-done((bf16[1,432,512]{2,1,0:T(8,128)(2,1)S(1)}, bf16[1,432,512]{2,1,0:T(8,128)(2,1)S(1)}, u32[]{:S(2)}, u32[]{:S(2)}) %collective-permute-start.11) | collective-permute-done | bytes 442400 | tf_op jit(solution)/shard_map/ppermute | solution.py:733
  300.8 2.0 dynamic_update_slice.7
  304.4 3.4 %shard_map.294 = f32[96,8,512]{2,1,0:T(8,128)} custom-call(f32[768,512]{1,0:T(8,128)} %get-tuple-element.40.dx1, bf16[8,96,512]{2,1,0:T(8,128)(2,1)} %copy-done.5), custom_call_target="tpu_custom_call" | custom-call | tf_op jit(solution)/shard_map/pallas_call | solution.py:84
  307.9 1.9 collective-permute-done.12
  (81 shorter events, 33.1 us)
Async XLA Ops:
  32.6 4.8 %copy-start = (bf16[8,104,512]{2,1,0:T(8,128)(2,1)}, bf16[8,104,512]{2,1,0:T(8,128)(2,1)S(1)}, u32[]{:S(2)}) copy-start(bf16[8,104,512]{2,1,0:T(8,128)(2,1)S(1)} %all_to_all.20.refs_0_.refs_2_) | copy-start | bytes 2555908
  32.6 4.8 %collective-permute-start = (bf16[8,104,512]{2,1,0:T(8,128)(2,1)S(1)}, bf16[8,104,512]{2,1,0:T(8,128)(2,1)S(1)}, u32[]{:S(2)}, u32[]{:S(2)}) collective-permute-start(bf16[8,104,512]{2,1,0:T(8,128)(2,1)S(1)} %all_to_all.20.refs_0_.refs_2_), channel_id=1, source_target_pairs={{0,1},{1,0},{2,3},{3,2},{4,5},{5,4},{6,7},{7,6},{8,9},{9,8},{10,11... | collective-permute-start | bytes 2555912 | tf_op jit(solution)/shard_map/ppermute | solution.py:805
  34.9 0.7 copy-start.6
  34.9 35.0 %copy-start.3 = (bf16[512,256]{1,0:T(8,128)(2,1)}, bf16[512,256]{1,0:T(8,128)(2,1)S(1)}, u32[]{:S(2)}) copy-start(bf16[512,256]{1,0:T(8,128)(2,1)S(1)} %get-tuple-element.62.wv) | copy-start | bytes 786436
  37.3 0.9 copy-start.7
  143.9 6.8 %collective-permute-start.8 = (bf16[8,432,512]{2,1,0:T(8,128)(2,1)}, bf16[8,432,512]{2,1,0:T(8,128)(2,1)S(1)}, u32[]{:S(2)}, u32[]{:S(2)}) collective-permute-start(bf16[8,432,512]{2,1,0:T(8,128)(2,1)} %get-tuple-element.59), channel_id=1, source_target_pairs={{0,1},{1,0},{2,3},{3,2},{4,5},{5,4},{6,7},{7,6},{8,9},{9,8},{10,11... | collective-permute-start | bytes 10616840 | tf_op jit(solution)/shard_map/ppermute | solution.py:733
  144.7 26.9 %all-to-all-start.2 = ((bf16[16,96,256]{2,1,0:T(8,128)(2,1)}), bf16[16,96,256]{2,1,0:T(8,128)(2,1)}, u32[]{:S(2)}, u32[]{:S(2)}) async-start(bf16[16,96,256]{2,1,0:T(8,128)(2,1)} %get-tuple-element.42), calls=%async_computation.2 | async-start | bytes 1572864 | tf_op jit(solution)/shard_map/all_to_all | solution.py:899
  150.7 1.7 copy-start.4
  157.9 70.4 %collective-permute-start.9 = (bf16[4,432,512]{2,1,0:T(8,128)(2,1)}, bf16[4,432,512]{2,1,0:T(8,128)(2,1)}, u32[]{:S(2)}, u32[]{:S(2)}) collective-permute-start(bf16[4,432,512]{2,1,0:T(8,128)(2,1)} %slice.144), channel_id=1, source_target_pairs={{0,2},{1,3},{2,0},{3,1},{4,6},{5,7},{6,4},{7,5},{8,10},{9,11},{10,... | collective-permute-start | bytes 5308424 | tf_op jit(solution)/shard_map/ppermute | solution.py:733
  202.2 24.9 %collective-permute-start.2 = (bf16[4,80,768]{2,1,0:T(8,128)(2,1)}, bf16[4,80,768]{2,1,0:T(8,128)(2,1)S(1)}, u32[]{:S(2)}, u32[]{:S(2)}) collective-permute-start(bf16[4,80,768]{2,1,0:T(8,128)(2,1)} %get-tuple-element.57), channel_id=1, source_target_pairs={{0,8},{1,9},{2,10},{3,11},{4,12},{5,13},{6,14},{7,15},{8,0},{9,1},... | collective-permute-start | bytes 1474568 | tf_op jit(solution)/shard_map/ppermute | solution.py:733
  203.8 40.9 %collective-permute-start.1 = (bf16[8,96,512]{2,1,0:T(8,128)(2,1)}, bf16[8,96,512]{2,1,0:T(8,128)(2,1)}, u32[]{:S(2)}, u32[]{:S(2)}) collective-permute-start(bf16[8,96,512]{2,1,0:T(8,128)(2,1)} %get-tuple-element.55), channel_id=1, source_target_pairs={{0,1},{1,0},{2,3},{3,2},{4,5},{5,4},{6,7},{7,6},{8,9},{9,8},{10,11... | collective-permute-start | bytes 2359304 | tf_op jit(solution)/shard_map/ppermute | solution.py:960
  228.2 9.3 %collective-permute-start.3 = (bf16[2,80,768]{2,1,0:T(8,128)(2,1)S(1)}, bf16[2,80,768]{2,1,0:T(8,128)(2,1)S(1)}, u32[]{:S(2)}, u32[]{:S(2)}) collective-permute-start(bf16[2,80,768]{2,1,0:T(8,128)(2,1)S(1)} %slice.135), channel_id=1, source_target_pairs={{0,4},{1,5},{2,6},{3,7},{4,0},{5,1},{6,2},{7,3},{8,12},{9,13},{10,... | collective-permute-start | bytes 737288 | tf_op jit(solution)/shard_map/ppermute | solution.py:733
  230.3 1.2 copy-start.1
  231.6 51.0 %collective-permute-start.10 = (bf16[2,432,512]{2,1,0:T(8,128)(2,1)S(1)}, bf16[2,432,512]{2,1,0:T(8,128)(2,1)}, u32[]{:S(2)}, u32[]{:S(2)}) collective-permute-start(bf16[2,432,512]{2,1,0:T(8,128)(2,1)S(1)} %slice.146), channel_id=1, source_target_pairs={{0,8},{1,9},{2,10},{3,11},{4,12},{5,13},{6,14},{7,15},{8,0},{9,1},... | collective-permute-start | bytes 2654216 | tf_op jit(solution)/shard_map/ppermute | solution.py:733
  237.6 4.9 %collective-permute-start.4 = (bf16[1,80,768]{2,1,0:T(8,128)(2,1)S(1)}, bf16[1,80,768]{2,1,0:T(8,128)(2,1)S(1)}, u32[]{:S(2)}, u32[]{:S(2)}) collective-permute-start(bf16[1,80,768]{2,1,0:T(8,128)(2,1)S(1)} %slice.137), channel_id=1, source_target_pairs={{0,2},{1,3},{2,0},{3,1},{4,6},{5,7},{6,4},{7,5},{8,10},{9,11},{10,... | collective-permute-start | bytes 368648 | tf_op jit(solution)/shard_map/ppermute | solution.py:733
  243.2 9.1 %collective-permute-start.5 = (bf16[80,768]{1,0:T(8,128)(2,1)}, bf16[80,768]{1,0:T(8,128)(2,1)}, u32[]{:S(2)}, u32[]{:S(2)}) collective-permute-start(bf16[80,768]{1,0:T(8,128)(2,1)} %fusion.2), channel_id=1, source_target_pairs={{0,16},{16,0},{1,17},{17,1},{2,18},{18,2},{3,19},{19,3},{4,20},{20... | collective-permute-start | bytes 368648 | tf_op jit(solution)/shard_map/ppermute | solution.py:743
  248.3 34.3 %copy-start.2 = (bf16[4,432,512]{2,1,0:T(8,128)(2,1)S(1)}, bf16[4,432,512]{2,1,0:T(8,128)(2,1)}, u32[]{:S(2)}) copy-start(bf16[4,432,512]{2,1,0:T(8,128)(2,1)} %copy-done.1) | copy-start | bytes 5308420
  248.3 55.3 %all-to-all-start.3 = ((bf16[8,96,512]{2,1,0:T(8,128)(2,1)}), bf16[8,96,512]{2,1,0:T(8,128)(2,1)S(1)}, u32[]{:S(2)}, u32[]{:S(2)}) async-start(bf16[8,96,512]{2,1,0:T(8,128)(2,1)} %shard_map.293), calls=%async_computation.3 | async-start | bytes 1572864 | tf_op jit(solution)/shard_map/all_to_all | solution.py:969
  254.6 29.5 %copy-start.8 = (bf16[2,32,3,256]{3,2,1,0:T(4,128)(2,1)S(1)}, bf16[2,32,3,256]{3,2,1,0:T(4,128)(2,1)}, u32[]{:S(2)}) copy-start(bf16[2,32,3,256]{3,2,1,0:T(4,128)(2,1)} %reshape.93) | copy-start | bytes 294916
  284.0 14.4 %collective-permute-start.11 = (bf16[1,432,512]{2,1,0:T(8,128)(2,1)S(1)}, bf16[1,432,512]{2,1,0:T(8,128)(2,1)S(1)}, u32[]{:S(2)}, u32[]{:S(2)}) collective-permute-start(bf16[1,432,512]{2,1,0:T(8,128)(2,1)S(1)} %slice.148), channel_id=1, source_target_pairs={{0,4},{1,5},{2,6},{3,7},{4,0},{5,1},{6,2},{7,3},{8,12},{9,13},{10,... | collective-permute-start | bytes 1327112 | tf_op jit(solution)/shard_map/ppermute | solution.py:733
  284.2 16.6 %collective-permute-start.7 = (bf16[32,3,256]{2,0,1:T(8,128)(2,1)S(1)}, bf16[32,3,256]{2,0,1:T(8,128)(2,1)S(1)}, u32[]{:S(2)}, u32[]{:S(2)}) collective-permute-start(bf16[32,3,256]{2,0,1:T(8,128)(2,1)S(1)} %bitcast.51), channel_id=1, source_target_pairs={{0,1},{1,0},{2,3},{3,2},{4,5},{5,4},{6,7},{7,6},{8,9},{9,8},{10,11... | collective-permute-start | bytes 147464 | tf_op jit(solution)/shard_map/ppermute | solution.py:989
  285.1 15.1 %collective-permute-start.6 = (bf16[8,512]{1,0:T(8,128)(2,1)S(1)}, bf16[8,512]{1,0:T(8,128)(2,1)S(1)}, u32[]{:S(2)}, u32[]{:S(2)}) collective-permute-start(bf16[8,512]{1,0:T(8,128)(2,1)S(1)} %pad_maximum_fusion.3), channel_id=1, source_target_pairs={{0,1},{1,0},{2,3},{3,2},{4,5},{5,4},{6,7},{7,6},{8,9},{9,8},{10,11... | collective-permute-start | bytes 24584 | tf_op jit(solution)/shard_map/ppermute | solution.py:995
  298.6 11.2 %collective-permute-start.12 = (bf16[432,512]{1,0:T(8,128)(2,1)S(1)}, bf16[432,512]{1,0:T(8,128)(2,1)S(1)}, u32[]{:S(2)}, u32[]{:S(2)}) collective-permute-start(bf16[432,512]{1,0:T(8,128)(2,1)S(1)} %fusion), channel_id=1, source_target_pairs={{0,16},{16,0},{1,17},{17,1},{2,18},{18,2},{3,19},{19,3},{4,20},{20... | collective-permute-start | bytes 1327112 | tf_op jit(solution)/shard_map/ppermute | solution.py:743
  303.5 0.9 copy-start.5
  (1 other events, 0.7 us)

commit v2 on v1

v2 whole, which is shorter than its diff:
```python
import functools
import math

import jax
import jax.numpy as jnp
from jax import lax
from jax.experimental import pallas as pl
from jax.experimental.pallas import tpu as pltpu
from jax.sharding import PartitionSpec as P

H = 8
HD = 64
EPSILON = 1e-05
SCALING = 0.125
NEGATIVE = -1e30
BF = jnp.bfloat16
F32 = jnp.float32
TILE = 256
PB = 512
KB = 256
QB = 256
TQ = 256
TK = 256
LANES = 128
PAD = 8
GELU_C = math.sqrt(2.0 / math.pi)
GELU_A = 0.044715
VMEM_LIMIT = 60 * 1024 * 1024
CLASSES = 5


def dot(a, b):
    return jnp.dot(a, b, preferred_element_type=F32)


def dot_nt(a, b):
    return lax.dot_general(a, b, (((1,), (1,)), ((), ())), preferred_element_type=F32)


def dot_tn(a, b):
    return lax.dot_general(a, b, (((0,), (0,)), ((), ())), preferred_element_type=F32)


def ln_parts(v):
    c = v - jnp.mean(v, -1, keepdims=True)
    r = lax.rsqrt(jnp.mean(c * c, -1, keepdims=True) + EPSILON)
    return c * r, r


def ln_back(dh, n, r, g):
    e = dh * g
    return r * (e - jnp.mean(e, -1, keepdims=True) - n * jnp.mean(e * n, -1, keepdims=True))


def flip(v):
    return jnp.transpose(v)


def head_columns(w, r, cl, which):
    first = which * (w.shape[1] // 3) + r * cl
    return w[:, pl.ds(pl.multiple_of(first, LANES), cl)]


def lay(scr, v):
    for a in range(scr.shape[0]):
        scr[a] = v[:, a * LANES : (a + 1) * LANES]


def lift(scr):
    return jnp.concatenate([scr[a] for a in range(scr.shape[0])], -1)


def take(scr, first, count, step):
    return jnp.concatenate(
        [scr[a, pl.ds(first, count, stride=step), :] for a in range(scr.shape[0])], -1
    )


def place(scr, first, count, step, v):
    for a in range(scr.shape[0]):
        scr[a, pl.ds(first, count, stride=step), :] = v[:, a * LANES : (a + 1) * LANES]


def iota(shape, dim):
    return lax.broadcasted_iota(jnp.int32, shape, dim).astype(F32)


def call(fn, outs, scratch, *args, smem=(), smem_out=()):
    def spec(space):
        return pl.BlockSpec(memory_space=space)

    in_specs = [spec(pltpu.SMEM if i in smem else pltpu.VMEM) for i in range(len(args))]
    out_specs = [spec(pltpu.SMEM if i in smem_out else pltpu.VMEM) for i in range(len(outs))]
    return pl.pallas_call(
        fn,
        out_shape=[jax.ShapeDtypeStruct(*o) for o in outs],
        in_specs=in_specs,
        out_specs=out_specs,
        scratch_shapes=scratch,
        compiler_params=pltpu.CompilerParams(vmem_limit_bytes=VMEM_LIMIT),
        cost_estimate=pl.CostEstimate(flops=0, bytes_accessed=0, transcendentals=0),
    )(*args)


def pack_kernel(tok, seg, out, scr):
    count, feats, width = tok.shape
    lay(scr, tok[...].astype(F32).reshape(count * feats, width))
    row = seg[...].astype(F32)
    for f in range(feats):
        out[f, :count, :] = take(scr, f, count, feats).astype(BF)
        out[f, count:, :] = jnp.zeros((PAD, width), BF)
        out[f, count:, :count] = jnp.broadcast_to(row, (PAD, count)).astype(BF)


def codes(pos, starts):
    cls = jnp.zeros_like(pos)
    for st in starts:
        cls = cls + jnp.where(pos >= st, 1.0, 0.0)
    return jnp.where(cls >= CLASSES - 1, pos + CLASSES, cls)


def tile_range(start_ref, first, size, tile):
    last = first + size - 1
    lo = jnp.int32(0)
    hi = start_ref[1]
    for c in range(1, CLASSES - 1):
        st = start_ref[c]
        lo = jnp.where(first >= st, st, lo)
        hi = jnp.where(last >= st, start_ref[c + 1], hi)
    pad = start_ref[CLASSES - 1]
    lo = jnp.where(first >= pad, first, lo)
    hi = jnp.where(last >= pad, first + size, hi)
    return lo // tile, (hi + tile - 1) // tile


def permute_block(rank_row, first, rows, total):
    pos = iota((rows, LANES), 0) + first.astype(F32)
    parts = []
    for j in range(total // LANES):
        hit = rank_row[0:1, j * LANES : (j + 1) * LANES] == pos
        parts.append(jnp.where(hit, 1.0, 0.0).astype(BF))
    return jnp.concatenate(parts, -1)


def unpermute_block(rank_col, total):
    rows = rank_col.shape[0]
    parts = []
    for j in range(total // LANES):
        pos = iota((1, LANES), 1) + float(j * LANES)
        parts.append(jnp.where(rank_col == pos, 1.0, 0.0).astype(BF))
    return jnp.concatenate(parts, -1)


def fwd_kernel(hpd, hl, r_ref, *refs):
    xparts = refs[:hpd]
    (g1, b1, w_in) = refs[hpd : hpd + 3]
    (o_send, xs_out, ot_out, lse_out, rank_row, rank_col, start_ref) = refs[hpd + 3 : hpd + 10]
    (x_scr, seg_scr, qtz, k_scr, vt, o_scr, code_col, code_row, acc, top, s_scr) = refs[
        hpd + 10 : hpd + 21
    ]
    wqt, wvt = refs[hpd + 21 :]
    feats = xparts[0].shape[0]
    count = xparts[0].shape[1] - PAD
    total = x_scr.shape[0]
    cl = hl * HD
    r = r_ref[0]
    chunks = total // LANES
    wqt[...] = flip(head_columns(w_in, r, cl, 0)) * BF(SCALING)
    wvt[...] = flip(head_columns(w_in, r, cl, 2))

    for s in range(hpd):
        for k in range(feats):
            at = (s * feats + k) * count
            x_scr[at : at + count, :] = xparts[s][k, :count, :]
            row = xparts[s][k, count : count + PAD, :LANES].astype(F32)[0:1]
            col = jnp.transpose(jnp.broadcast_to(row, (LANES, LANES)))
            seg_scr[at : at + count, :] = col[:count, :]

    seg = seg_scr[...]
    cls = jnp.where(seg < 0.0, float(CLASSES - 1), seg)
    seg_scr[...] = cls * 8192.0 + iota((total, LANES), 0)
    key_rows = []
    for j in range(chunks):
        blk = seg_scr[j * LANES : (j + 1) * LANES, :]
        key_rows.append(jnp.transpose(blk)[0:8, :])

    def count_less(i, carry):
        blk = seg_scr[pl.ds(pl.multiple_of(i * 64, 64), 64), :]
        out = []
        for j in range(chunks):
            less = jnp.where(blk < key_rows[j][0:1], 1.0, 0.0)
            out.append(carry[j] + jnp.sum(less.reshape(8, 8, LANES), 0))
        return tuple(out)

    ranks = lax.fori_loop(
        0, total // 64, count_less, tuple(jnp.zeros((8, LANES), F32) for _ in range(chunks))
    )
    for j in range(chunks):
        row = jnp.sum(ranks[j], 0, keepdims=True)
        rank_row[:, j * LANES : (j + 1) * LANES] = jnp.broadcast_to(row, (8, LANES))
        rank_col[j * LANES : (j + 1) * LANES, :] = jnp.transpose(
            jnp.broadcast_to(row, (LANES, LANES))
        )
    starts = []
    keys = jnp.concatenate([k[0:1] for k in key_rows], 0)
    for c in range(1, CLASSES):
        st = jnp.sum(jnp.where(keys < c * 8192.0, 1.0, 0.0))
        starts.append(st)
        start_ref[c] = st.astype(jnp.int32)
    start_ref[0] = jnp.int32(0)
    for c in range(CLASSES, 8):
        start_ref[c] = jnp.int32(total)
    code_col[...] = codes(iota((total, LANES), 0), starts)
    code_row[...] = codes(iota((8, total), 1), starts)

    qtz[...] = jnp.zeros_like(qtz)
    ones = jnp.where(iota((16, total), 0) == 0.0, 1.0, 0.0).astype(BF)
    for h in range(hl):
        vt[h, HD:, :] = ones

    def project(b, _):
        at = pl.multiple_of(b * PB, PB)
        block = dot(permute_block(rank_row, at, PB, total), x_scr[...])
        xs_out[pl.ds(at, PB), :] = block.astype(BF)
        n, _r = ln_parts(block)
        h1 = (n * g1[...] + b1[...]).astype(BF)
        qt = dot_nt(wqt[...], h1).astype(BF)
        k_scr[pl.ds(at, PB), :] = dot(h1, head_columns(w_in, r, cl, 1)).astype(BF)
        vv = dot_nt(wvt[...], h1).astype(BF)
        for h in range(hl):
            sub = (h % 2) * HD
            qtz[h, sub : sub + HD, pl.ds(at, PB)] = qt[h * HD : (h + 1) * HD]
            vt[h, :HD, pl.ds(at, PB)] = vv[h * HD : (h + 1) * HD]
        return 0

    lax.fori_loop(0, total // PB, project, 0)

    def attend(b, _):
        at = pl.multiple_of(b * TQ, TQ)
        t0, t1 = tile_range(start_ref, at, TQ, TK)
        acc[...] = jnp.zeros_like(acc)
        top[...] = jnp.full_like(top, NEGATIVE)
        crow = code_row[0:1, pl.ds(at, TQ)]

        def score(t, _):
            kt = pl.multiple_of(t * TK, TK)
            ccol = code_col[pl.ds(kt, TK), :]
            ccol = jnp.concatenate([ccol] * (TQ // LANES), -1)
            seen = ccol == crow
            for h in range(hl):
                pair = (h // 2) * LANES
                s = dot(k_scr[pl.ds(kt, TK), pair : pair + LANES], qtz[h, :, pl.ds(at, TQ)])
                s = jnp.where(seen, s, NEGATIVE)
                s_scr[h, pl.ds(kt, TK), :] = s
                top[h] = jnp.maximum(top[h], jnp.max(s.reshape(TK // 8, 8, TQ), 0))
            return 0

        lax.fori_loop(t0, t1, score, 0)
        for h in range(hl):
            top[h] = jnp.broadcast_to(jnp.max(top[h], 0, keepdims=True), (8, TQ))

        def mix(t, _):
            kt = pl.multiple_of(t * TK, TK)
            for h in range(hl):
                p = jnp.exp(s_scr[h, pl.ds(kt, TK), :] - top[h, 0:1, :]).astype(BF)
                acc[h] += dot(vt[h, :, pl.ds(kt, TK)], p)
            return 0

        lax.fori_loop(t0, t1, mix, 0)
        outs = []
        for h in range(hl):
            total_h = acc[h, HD : HD + 1, :]
            outs.append(acc[h, :HD, :] / total_h)
            lse_out[h : h + 1, pl.ds(at, TQ)] = top[h, 0:1, :] + jnp.log(total_h)
        ot = jnp.concatenate(outs, 0)
        ot_out[:, pl.ds(at, TQ)] = ot.astype(BF)
        o_scr[pl.ds(at, TQ), :] = jnp.transpose(ot).astype(BF)
        return 0

    lax.fori_loop(0, total // TQ, attend, 0)

    group = feats // 2
    for blk in range(total // (group * count)):
        at = blk * group * count
        hot = unpermute_block(rank_col[at : at + group * count, :], total)
        o = dot(hot, o_scr[...]).astype(BF)
        for j in range(group):
            s, k = divmod(blk * group + j, feats)
            dest = k * hpd + lax.rem(r - s + hpd, hpd)
            o_send[dest] = o[j * count : (j + 1) * count]


def prep_kernel(
    hl,
    r_ref,
    xs,
    g1,
    b1,
    w_in,
    k_out,
    v_out,
    kt_out,
    qtz,
    nt,
    wqt,
    wkt,
):
    total = xs.shape[0]
    cl = hl * HD
    r = r_ref[0]
    wqt[...] = flip(head_columns(w_in, r, cl, 0)) * BF(SCALING)
    wkt[...] = flip(head_columns(w_in, r, cl, 1))
    qtz[...] = jnp.zeros_like(qtz)

    def project(b, _):
        at = pl.multiple_of(b * PB, PB)
        n, _r = ln_parts(xs[pl.ds(at, PB), :].astype(F32))
        h1 = (n * g1[...] + b1[...]).astype(BF)
        nt[:, pl.ds(at, PB)] = jnp.transpose(n.astype(BF))
        qt = dot_nt(wqt[...], h1).astype(BF)
        k_out[pl.ds(at, PB), :] = dot(h1, head_columns(w_in, r, cl, 1)).astype(BF)
        v_out[pl.ds(at, PB), :] = dot(h1, head_columns(w_in, r, cl, 2)).astype(BF)
        kt_out[:, pl.ds(at, PB)] = dot_nt(wkt[...], h1).astype(BF)
        for h in range(hl):
            sub = (h % 2) * HD
            qtz[h, sub : sub + HD, pl.ds(at, PB)] = qt[h * HD : (h + 1) * HD]
        return 0

    lax.fori_loop(0, total // PB, project, 0)


def add_all(terms):
    total = terms[0].astype(F32)
    for term in terms[1:]:
        total = total + term.astype(F32)
    return total.astype(BF)


def bwd_kernel(
    hpd,
    hl,
    r_ref,
    start_ref,
    do_recv,
    k_in,
    v_in,
    kt_in,
    qtz,
    ot,
    lse,
    rank_row,
    dt_out,
    do_scr,
    dotz,
    dots,
    code_col,
    code_row,
    dq_acc,
    dk_acc,
    dv_acc,
    p_scr,
    ds_scr,
    pairs,
):
    feats = do_recv.shape[0] // hpd
    count = do_recv.shape[1]
    total = do_scr.shape[0]
    cl = hl * HD
    r = r_ref[0]

    for s in range(hpd):
        for k in range(feats):
            at = (s * feats + k) * count
            do_scr[at : at + count, :] = do_recv[k * hpd + lax.rem(r - s + hpd, hpd)]
    starts = [start_ref[c].astype(F32) for c in range(1, CLASSES)]
    code_col[...] = codes(iota((total, LANES), 0), starts)
    code_row[...] = codes(iota((8, total), 1), starts)
    dotz[...] = jnp.zeros_like(dotz)

    def arrange(b, _):
        at = pl.multiple_of(b * PB, PB)
        block = jnp.transpose(dot(permute_block(rank_row, at, PB, total), do_scr[...]))
        prod = block * ot[:, pl.ds(at, PB)].astype(F32)
        for h in range(hl):
            sub = (h % 2) * HD
            rows = slice(h * HD, (h + 1) * HD)
            dotz[h, sub : sub + HD, pl.ds(at, PB)] = block[rows].astype(BF)
            dots[h : h + 1, pl.ds(at, PB)] = jnp.sum(prod[rows], 0, keepdims=True)
        return 0

    lax.fori_loop(0, total // PB, arrange, 0)
    dq_acc[...] = jnp.zeros_like(dq_acc)
    dk_acc[...] = jnp.zeros_like(dk_acc)
    dv_acc[...] = jnp.zeros_like(dv_acc)

    def list_keys(b, filled):
        t0, t1 = tile_range(start_ref, b * KB, KB, QB)

        def put(t, i):
            pairs[i] = b * 4096 + t
            return i + 1

        return lax.fori_loop(t0, t1, put, filled)

    filled = lax.fori_loop(0, total // KB, list_keys, jnp.int32(0))

    def places(i):
        b, t = pairs[i] // 4096, lax.rem(pairs[i], 4096)
        return pl.ds(pl.multiple_of(b * KB, KB), KB), pl.ds(pl.multiple_of(t * QB, QB), QB)

    def scores(i):
        kt, at = places(i)
        ccol = code_col[kt, :]
        seen = jnp.concatenate([ccol] * (QB // LANES), -1) == code_row[0:1, at]
        for h in range(hl):
            cols = slice(h // 2 * LANES, (h // 2 + 1) * LANES)
            s = dot(k_in[kt, cols], qtz[h, :, at])
            p = jnp.where(seen, jnp.exp(s - lse[h : h + 1, at]), 0.0)
            dp = dot(v_in[kt, cols], dotz[h, :, at])
            p_scr[h] = p.astype(BF)
            ds_scr[h] = (p * (dp - dots[h : h + 1, at])).astype(BF)

    def collect(i):
        kt, at = places(i)
        for h in range(hl):
            rows = slice(h * HD, (h + 1) * HD)
            own = slice((h % 2) * HD, (h % 2 + 1) * HD)
            ds = ds_scr[h]
            dv_acc[rows, kt] += dot_nt(dotz[h, own, at], p_scr[h])
            dk_acc[rows, kt] += dot_nt(qtz[h, own, at], ds)
            dq_acc[rows, at] += dot(kt_in[rows, kt], ds)

    def step(i, _):
        scores(i)
        collect(i)
        return 0

    lax.fori_loop(0, filled, step, 0)
    dt_out[:cl, :] = (dq_acc[...] * SCALING).astype(BF)
    dt_out[cl : 2 * cl, :] = dk_acc[...].astype(BF)
    dt_out[2 * cl :, :] = dv_acc[...].astype(BF)


def dh_kernel(hpd, r_ref, dt, w_in, rank_col, *refs):
    dh_outs, dht = refs[: 2 * hpd], refs[2 * hpd]
    half, count, width = dh_outs[0].shape
    feats = 2 * half
    total = dt.shape[1]
    cl = dt.shape[0] // 3
    w3 = jnp.concatenate([head_columns(w_in, r_ref[0], cl, j) for j in range(3)], 1)
    for b in range(total // PB):
        at = slice(b * PB, (b + 1) * PB)
        dht[:, at] = dot(w3, dt[:, at]).astype(BF)
    group = feats // 2
    for blk in range(total // (group * count)):
        at = blk * group * count
        hot = unpermute_block(rank_col[at : at + group * count, :], total)
        o = dot_nt(hot, dht[...]).astype(BF)
        for j in range(group):
            s, k = divmod(blk * group + j, feats)
            dh_outs[2 * s + k // half][k % half] = o[j * count : (j + 1) * count]


SUB = 16


def q_rows(cl, width):
    return SUB * (-(-6 * cl // width)) + SUB


def dw_kernel(r_ref, x_ref, dt, nt, w_in, g1, b1, q_keep, q_send, m_scr, dw_scr):
    x = x_ref[0]
    width, total = nt.shape
    cols = dt.shape[0]
    cl = cols // 3
    feats = q_keep.shape[0]
    for c in range(3):
        rows = slice(c * cl, (c + 1) * cl)
        m_scr[:, rows] = dot_nt(nt[...], dt[rows, :])
    ones = jnp.ones((8, total), BF)
    sums_row = dot_nt(ones, dt[...])[0:1]
    gcol = jnp.transpose(jnp.broadcast_to(g1[...], (LANES, width)))
    bcol = jnp.transpose(jnp.broadcast_to(b1[...], (LANES, width)))
    gg = jnp.zeros((width, LANES), F32)
    gb = jnp.zeros((width, LANES), F32)
    for j in range(cols // LANES):
        lanes = slice(j * LANES, (j + 1) * LANES)
        first = (j * LANES // cl) * width + r_ref[0] * cl + j * LANES % cl
        w = w_in[:, pl.ds(pl.multiple_of(first, LANES), LANES)].astype(F32)
        m = m_scr[:, lanes]
        gg = gg + w * m
        gb = gb + w * sums_row[:, lanes]
        dw_scr[:, lanes] = (m * gcol + bcol * sums_row[:, lanes]).astype(BF)
    gg = jnp.sum(jnp.transpose(gg), 0, keepdims=True)
    gb = jnp.sum(jnp.transpose(gb), 0, keepdims=True)
    vec = jnp.concatenate([gg, gb, jnp.zeros((SUB - 2, width), F32)], 0).astype(BF)
    per = width // cl
    last = q_keep.shape[1] - SUB
    for e in range(feats):
        for ref, side in ((q_keep, x), (q_send, 1 - x)):
            for s in range(6):
                j, b = divmod(s, 2)
                src = pl.multiple_of((e * 4 + b) * SUB + side * 2 * SUB, SUB)
                to = (s // per) * SUB
                ref[e, to : to + SUB, (s % per) * cl : (s % per + 1) * cl] = dw_scr[
                    pl.ds(src, SUB), j * cl : (j + 1) * cl
                ]
            used = 6 % per
            if used:
                ref[e, last - SUB : last, used * cl :] = jnp.zeros((SUB, width - used * cl), BF)
            ref[e, last:, :] = vec


def gather_kernel(hpd, r_ref, x_ref, *refs):
    same, other = refs[:hpd], refs[hpd : 2 * hpd]
    sums, got = refs[2 * hpd : 2 * hpd + 2]
    out, vec, down, up, fqkv, fout, sout, vectors = refs[2 * hpd + 2 :]
    piece = out.shape[0]
    rows, width = same[0].shape
    cl = width // hpd
    r, x = r_ref[0], x_ref[0]
    blocks = piece // SUB
    first = lax.rem(r * blocks, 2)
    from_same = r * blocks // 2 == x
    for s in range(hpd):
        owner = lax.rem(r - s + hpd, hpd)
        for j in range(3):
            lo = 2 * j // hpd * SUB
            to = pl.ds(pl.multiple_of(j * width + owner * cl, LANES), cl)
            for b in range(blocks):
                col = pl.multiple_of((2 * j % hpd + first + b) * cl, LANES)
                at = (slice(lo, lo + SUB), pl.ds(col, cl))
                picked = jnp.where(from_same, same[s][at].astype(F32), other[s][at].astype(F32))
                out[b * SUB : (b + 1) * SUB, to] = picked
    total = same[0][rows - SUB : rows, :].astype(F32)
    for s in range(1, hpd):
        total = total + same[s][rows - SUB : rows, :].astype(F32)
    vec[...] = total[:8]

    def both(first, size):
        at = slice(first, first + size)
        return sums[at, :].astype(F32) + got[at, :].astype(F32)

    down[...] = both(0, down.shape[0])
    base = down.shape[0]
    for ref in (up, fqkv, fout, sout):
        for b in range(ref.shape[1] // width):
            ref[:, b * width : (b + 1) * width] = both(base, piece)
            base += piece
    vectors[...] = both(base, vectors.shape[0])


def norm_kernel(hpd, *refs):
    parts = refs[: 2 * hpd]
    x, g1, q_keep, q_got, out = refs[2 * hpd :]
    half, count, _w = parts[0].shape
    feats = 2 * half
    for k in range(feats):
        dh = parts[k // half][k % half].astype(F32)
        for s in range(1, hpd):
            dh = dh + parts[2 * s + k // half][k % half].astype(F32)
        n, r = ln_parts(x[k, :count, :].astype(F32))
        out[k, :count, :] = ln_back(dh, n, r, g1[...]).astype(BF)
        out[k, count:, :] = add_all((q_keep[k], q_got[k]))


def final_kernel(dx1, both, out, q_sum, scr):
    feats = both.shape[0]
    count, _f, width = out.shape
    q_sum[...] = add_all([both[k, count:, :] for k in range(feats)])
    for f in range(feats):
        val = dx1[f * count : (f + 1) * count, :] + both[f, :count, :].astype(F32)
        place(scr, f, count, feats, val)
    out[...] = lift(scr).reshape(count, feats, width)


def rows_kernel(
    hpd,
    o_recv,
    xt,
    cot,
    g2,
    b2,
    g3,
    b3,
    ub,
    db,
    wso,
    wfq,
    wfo,
    wup,
    wdn,
    out,
    dx1,
    do_send,
    sums,
    wide,
    ct,
    o1,
    x1,
    h2,
    qkv,
    o2,
    x2,
    h3,
    u,
    dz,
    dx2,
    do2,
    dqkv,
    pscr,
    tr,
    wblk,
    ubg,
    wdn_scr,
):
    feats = xt.shape[0]
    count = xt.shape[1] - PAD
    width = xt.shape[2]
    rows = feats * count
    hidden = wup.shape[1]
    n = o_recv.shape[0]
    cl = o_recv.shape[2]
    half = rows // 2
    lane = iota((1, LANES), 1)
    part = 16
    tiles = count // part
    size = feats * part

    lay(wide, cot[...].astype(F32).reshape(rows, width))
    for f in range(feats):
        ct[f * count : (f + 1) * count, :] = take(wide, f, count, feats).astype(BF)
        for c in range(hpd):
            o1[f * count : (f + 1) * count, c * cl : (c + 1) * cl] = o_recv[f * hpd + c]

    for b in range(2):
        at = slice(b * half, (b + 1) * half)
        x = xt[b * feats // 2 : (b + 1) * feats // 2, :count, :].astype(F32).reshape(half, width)
        v = x + dot(o1[at, :], wso[...])
        x1[at, :] = v
        nn, _r = ln_parts(v)
        h2[at, :] = (nn * g2[...] + b2[...]).astype(BF)

    qkv3 = qkv

    def qkv_step(c, _):
        cols = pl.ds(pl.multiple_of(c * TILE, TILE), TILE)
        scale = jnp.where(c < width // TILE, SCALING, 1.0)
        y = dot(h2[...], wfq[:, cols])
        qkv3[:, :, cols] = (y * scale).astype(BF).reshape(feats, count, TILE)
        return 0

    lax.fori_loop(0, 3 * width // TILE, qkv_step, 0)

    ri = lax.broadcasted_iota(jnp.int32, (2 * size, size), 0)
    ci = lax.broadcasted_iota(jnp.int32, (2 * size, size), 1)
    same = lax.rem(ri, part) == lax.rem(ci, part)
    low_lane = jnp.where(iota((1, LANES), 1) < HD, 1.0, 0.0).astype(BF)
    high_lane = jnp.where(iota((1, LANES), 1) < HD, 0.0, 1.0).astype(BF)

    def tile_of(ref, at, lo):
        return ref[:, at, lo : lo + LANES].reshape(size, LANES)

    def by_head(v):
        return jnp.concatenate([v * low_lane, v * high_lane], 0)

    def by_head_t(v):
        vt = jnp.transpose(v)
        zero = jnp.zeros((HD, size), BF)
        return jnp.concatenate(
            [jnp.concatenate([vt[:HD], zero], 0), jnp.concatenate([zero, vt[HD:]], 0)], 1
        )

    def side(v):
        return jnp.concatenate([v[:size], v[size:]], 1)

    def per_head(v, fn):
        return jnp.concatenate(
            [jnp.broadcast_to(fn(v[i * size : (i + 1) * size]), (size, size)) for i in (0, 1)], 0
        )

    def feat_fwd(t, _):
        at = pl.ds(pl.multiple_of(t * part, part), part)
        for p2 in range(H // 2):
            lo = p2 * LANES
            q = tile_of(qkv3, at, lo)
            k = tile_of(qkv3, at, width + lo)
            v = tile_of(qkv3, at, 2 * width + lo)
            s = jnp.where(same, dot_nt(by_head(k), q), NEGATIVE)
            e = jnp.exp(s - per_head(s, lambda w: jnp.max(w, 0, keepdims=True)))
            p = (e * per_head(e, lambda w: 1.0 / jnp.sum(w, 0, keepdims=True))).astype(BF)
            pscr[t, p2] = p
            ot = dot(by_head_t(v), p)
            o2[:, at, lo : lo + LANES] = jnp.transpose(ot).astype(BF).reshape(feats, part, LANES)
        return 0

    lax.fori_loop(0, tiles, feat_fwd, 0, unroll=True)

    for b in range(2):
        at = slice(b * half, (b + 1) * half)
        o = o2[b * feats // 2 : (b + 1) * feats // 2, :, :].reshape(half, width)
        v = x1[at, :] + dot(o, wfo[...])
        x2[at, :] = v
        nn, _r = ln_parts(v)
        h3[at, :] = (nn * g3[...] + b3[...]).astype(BF)

    def ffn(c, _):
        cols = pl.ds(pl.multiple_of(c * TILE, TILE), TILE)
        total = jnp.zeros((8, TILE), F32)
        for b in range(2):
            at = slice(b * half, (b + 1) * half)
            z = dot(h3[at, :], wup[:, cols]) + ub[0:1, cols]
            w = GELU_C * GELU_A * (z * z) + GELU_C
            cdf = 0.5 * jnp.tanh(z * w) + 0.5
            g = z * cdf
            u[at, cols] = g.astype(BF)
            slope = cdf + g * (1.0 - cdf) * (6.0 * w - 4.0 * GELU_C)
            d = dot_nt(ct[at, :], wdn[cols, :]) * slope
            dz[at, cols] = d.astype(BF)
            total = total + jnp.sum(d.reshape(half // 8, 8, TILE), 0)
        ubg[:, cols] = total
        return 0

    lax.fori_loop(0, hidden // TILE, ffn, 0)

    vectors = []
    gg = jnp.zeros((1, width), F32)
    gb = jnp.zeros((1, width), F32)
    gd = jnp.zeros((1, width), F32)
    for b in range(2):
        at = slice(b * half, (b + 1) * half)
        y = x2[at, :] + dot(u[at, :], wdn[...]) + db[...]
        for j in range(feats // 2):
            f = b * (feats // 2) + j
            place(wide, f, count, feats, y[j * count : (j + 1) * count])
        dh = dot_nt(dz[at, :], wup[...])
        nn, r = ln_parts(x2[at, :])
        c = ct[at, :].astype(F32)
        gg = gg + jnp.sum(dh * nn, 0, keepdims=True)
        gb = gb + jnp.sum(dh, 0, keepdims=True)
        gd = gd + jnp.sum(c, 0, keepdims=True)
        v = c + ln_back(dh, nn, r, g3[...])
        dx2[at, :] = v
        do2[b * feats // 2 : (b + 1) * feats // 2, :, :] = (
            dot_nt(v.astype(BF), wfo[...]).astype(BF).reshape(feats // 2, count, width)
        )
    out[...] = lift(wide).reshape(count, feats, width).astype(BF)
    vectors = [gg, gb, gd]

    def feat_bwd(t, _):
        at = pl.ds(pl.multiple_of(t * part, part), part)
        for p2 in range(H // 2):
            lo = p2 * LANES
            q = tile_of(qkv3, at, lo)
            k = tile_of(qkv3, at, width + lo)
            v = tile_of(qkv3, at, 2 * width + lo)
            g = tile_of(do2, at, lo)
            p = pscr[t, p2]
            pf = p.astype(F32)
            dp = dot_nt(by_head(v), g)
            ds = pf * (dp - per_head(pf * dp, lambda w: jnp.sum(w, 0, keepdims=True)))
            ds = ds.astype(BF)
            dv = dot(side(p), by_head(g))
            dk = dot(side(ds), by_head(q))
            dq = jnp.transpose(dot(by_head_t(k), ds)) * SCALING
            for j, d in enumerate((dq, dk, dv)):
                dqkv[:, at, j * width + lo : j * width + lo + LANES] = d.astype(BF).reshape(
                    feats, part, LANES
                )
        return 0

    lax.fori_loop(0, tiles, feat_bwd, 0, unroll=True)

    gg = jnp.zeros((1, width), F32)
    gb = jnp.zeros((1, width), F32)
    for b in range(2):
        at = slice(b * half, (b + 1) * half)
        d = dqkv[b * feats // 2 : (b + 1) * feats // 2, :, :].reshape(half, 3 * width)
        dh = dot_nt(d, wfq[...])
        nn, r = ln_parts(x1[at, :])
        gg = gg + jnp.sum(dh * nn, 0, keepdims=True)
        gb = gb + jnp.sum(dh, 0, keepdims=True)
        v = dx2[at, :] + ln_back(dh, nn, r, g2[...])
        dx1[at, :] = v
        g = dot_nt(v.astype(BF), wso[...]).astype(BF)
        for j in range(feats // 2):
            f = b * (feats // 2) + j
            for c in range(hpd):
                do_send[f * hpd + c] = g[j * count : (j + 1) * count, c * cl : (c + 1) * cl]
    vectors = [gg, gb] + vectors

    piece = width // n
    fpiece = hidden // n

    def spread(base):
        for d in range(n):
            sums[d, base : base + piece, :] = wblk[d * piece : (d + 1) * piece, :]

    base = 0
    for b in range(hidden // width):
        tr[...] = flip(u[:, b * width : (b + 1) * width])
        wdn_scr[b * width : (b + 1) * width, :] = dot(tr[...], ct[...]).astype(BF)
    for d in range(n):
        sums[d, base : base + fpiece, :] = wdn_scr[d * fpiece : (d + 1) * fpiece, :]
    base += fpiece
    tr[...] = flip(h3[...])
    for b in range(hidden // width):
        wblk[...] = dot(tr[...], dz[:, b * width : (b + 1) * width]).astype(BF)
        spread(base)
        base += piece
    tr[...] = flip(h2[...])
    for b in range(3):
        d = dqkv[:, :, b * width : (b + 1) * width].reshape(rows, width)
        wblk[...] = dot(tr[...], d).astype(BF)
        spread(base)
        base += piece
    tr[...] = flip(o2[...].reshape(rows, width))
    wblk[...] = dot(tr[...], dx2[...].astype(BF)).astype(BF)
    spread(base)
    base += piece
    tr[...] = flip(o1[...])
    wblk[...] = dot(tr[...], dx1[...].astype(BF)).astype(BF)
    spread(base)
    base += piece
    ubs = jnp.sum(ubg[...], 0, keepdims=True)
    vectors = vectors + [ubs[:, b * width : (b + 1) * width] for b in range(hidden // width)]
    vec = jnp.concatenate(vectors + [jnp.zeros((16 - len(vectors), width), F32)], 0).astype(BF)
    for d in range(n):
        sums[d, base : base + 16, :] = vec


def solution(mesh):
    n = mesh.shape["samp"]
    groups = mesh.shape["grp"]
    gbits = groups.bit_length() - 1
    tie = lax.optimization_barrier

    def swap_grp(v, bit=0):
        return lax.ppermute(v, "grp", [(d, d ^ (1 << bit)) for d in range(groups)])

    def rest_of_grp(v):
        for bit in range(1, gbits):
            v = (v.astype(F32) + swap_grp(v, bit).astype(F32)).astype(BF)
        return v

    def body(
        tokens,
        segments,
        cotangent,
        first_gain,
        first_shift,
        sample_qkv,
        sample_out,
        second_gain,
        second_shift,
        feature_qkv,
        feature_out,
        third_gain,
        third_shift,
        up_weight,
        up_bias,
        down_weight,
        down_bias,
    ):
        count, feats, width = tokens.shape[1:]
        hidden = up_weight.shape[1]
        rows = count * feats
        hpd = n // feats
        hl = H // hpd
        cl = hl * HD
        total = n * count
        heads8 = 8
        me = lax.axis_index("samp")
        r = lax.rem(me, hpd)
        x = lax.rem(lax.axis_index("grp"), 2)
        r1, x1 = (v.reshape(1).astype(jnp.int32) for v in (r, x))
        peers = [[q + hpd * k for k in range(feats)] for q in range(hpd)]
        g1, b1, g2, b2, g3, b3, ub, db = (
            v.reshape(1, -1)
            for v in (
                first_gain,
                first_shift,
                second_gain,
                second_shift,
                third_gain,
                third_shift,
                up_bias,
                down_bias,
            )
        )

        def shift(s):
            return [(d, d // hpd * hpd + (d % hpd + s) % hpd) for d in range(n)]

        (xt,) = call(
            pack_kernel,
            [((feats, count + PAD, width), BF)],
            [pltpu.VMEM((width // LANES, rows, LANES), F32)],
            tokens[0],
            segments,
        )
        mine = lax.all_to_all(xt, "samp", 0, 0, tiled=True, axis_index_groups=peers)
        xparts = [mine] + [lax.ppermute(mine, "samp", shift(s)) for s in range(1, hpd)]

        o_send, xs, ot, lse, rank_row, rank_col, starts = call(
            functools.partial(fwd_kernel, hpd, hl),
            [
                ((n, count, cl), BF),
                ((total, width), BF),
                ((cl, total), BF),
                ((heads8, total), F32),
                ((8, total), F32),
                ((total, LANES), F32),
                ((8,), jnp.int32),
            ],
            [
                pltpu.VMEM((total, width), BF),
                pltpu.VMEM((total, LANES), F32),
                pltpu.VMEM((hl, LANES, total), BF),
                pltpu.VMEM((total, cl), BF),
                pltpu.VMEM((hl, HD + 16, total), BF),
                pltpu.VMEM((total, cl), BF),
                pltpu.VMEM((total, LANES), F32),
                pltpu.VMEM((8, total), F32),
                pltpu.VMEM((hl, HD + 16, TQ), F32),
                pltpu.VMEM((hl, 8, TQ), F32),
                pltpu.VMEM((hl, total, TQ), F32),
                pltpu.VMEM((cl, width), BF),
                pltpu.VMEM((cl, width), BF),
            ],
            r1,
            *xparts,
            g1,
            b1,
            sample_qkv,
            smem=(0,),
            smem_out=(6,),
        )
        o_recv = lax.all_to_all(o_send, "samp", 0, 0, tiled=True)

        piece = width // n
        fpiece = hidden // n
        pieces = fpiece + piece * (hidden // width + 5) + 16
        vm = pltpu.VMEM
        out, dx1, do_send, sums = call(
            functools.partial(rows_kernel, hpd),
            [
                ((count, feats, width), BF),
                ((rows, width), F32),
                ((n, count, cl), BF),
                ((n, pieces, width), BF),
            ],
            [
                vm((width // LANES, rows, LANES), F32),
                vm((rows, width), BF),
                vm((rows, width), BF),
                vm((rows, width), F32),
                vm((rows, width), BF),
                vm((feats, count, 3 * width), BF),
                vm((feats, count, width), BF),
                vm((rows, width), F32),
                vm((rows, width), BF),
                vm((rows, hidden), BF),
                vm((rows, hidden), BF),
                vm((rows, width), F32),
                vm((feats, count, width), BF),
                vm((feats, count, 3 * width), BF),
                vm((count // 16, H // 2, 32 * feats, 16 * feats), BF),
                vm((width, rows), BF),
                vm((width, width), BF),
                vm((8, hidden), F32),
                vm((hidden, width), BF),
            ],
            o_recv,
            xt,
            cotangent[0],
            g2,
            b2,
            g3,
            b3,
            ub,
            db,
            sample_out,
            feature_qkv,
            feature_out,
            up_weight,
            down_weight,
        )
        sums = lax.psum_scatter(sums, "samp", scatter_dimension=0, tiled=True)[0]
        do_recv = lax.all_to_all(do_send, "samp", 0, 0, tiled=True)

        qr = q_rows(cl, width)
        k_all, v_all, kt_all, qtz, nt = call(
            functools.partial(prep_kernel, hl),
            [
                ((total, cl), BF),
                ((total, cl), BF),
                ((cl, total), BF),
                ((hl, LANES, total), BF),
                ((width, total), BF),
            ],
            [vm((cl, width), BF), vm((cl, width), BF)],
            r1,
            xs,
            g1,
            b1,
            sample_qkv,
            smem=(0,),
        )
        (dt,) = call(
            functools.partial(bwd_kernel, hpd, hl),
            [((3 * cl, total), BF)],
            [
                vm((total, cl), BF),
                vm((hl, LANES, total), BF),
                vm((8, total), F32),
                vm((total, LANES), F32),
                vm((8, total), F32),
                vm((cl, total), F32),
                vm((cl, total), F32),
                vm((cl, total), F32),
                vm((hl, KB, QB), BF),
                vm((hl, KB, QB), BF),
                pltpu.SMEM(((total // KB) * (total // QB),), jnp.int32),
            ],
            r1,
            starts,
            do_recv,
            k_all,
            v_all,
            kt_all,
            qtz,
            ot,
            lse,
            rank_row,
            smem=(0, 1),
        )
        q_keep, q_send = call(
            dw_kernel,
            [((feats, qr, width), BF)] * 2,
            [vm((width, 3 * cl), F32), vm((width, 3 * cl), BF)],
            r1,
            x1,
            dt,
            nt,
            sample_qkv,
            g1,
            b1,
            smem=(0, 1),
        )
        dt, _ = tie((dt, q_send))
        dhs = call(
            functools.partial(dh_kernel, hpd),
            [((feats // 2, count, width), BF)] * (2 * hpd),
            [vm((width, total), BF)],
            r1,
            dt,
            sample_qkv,
            rank_col,
            smem=(0,),
        )
        parts = list(dhs[:2])
        for s in range(1, hpd):
            parts += [lax.ppermute(v, "samp", shift(-s)) for v in dhs[2 * s : 2 * s + 2]]
        (both,) = call(
            functools.partial(norm_kernel, hpd),
            [((feats, count + qr, width), BF)],
            [],
            *parts,
            mine,
            g1,
            q_keep,
            swap_grp(q_send),
        )
        both_send = both
        both = lax.all_to_all(both, "samp", 0, 0, tiled=True, axis_index_groups=peers)
        dx1, _ = tie((dx1, both_send))
        sums, _ = tie((sums, both_send))
        sums = rest_of_grp(sums)
        sums_got = swap_grp(sums)
        grad_tokens, q_sum = call(
            final_kernel,
            [((count, feats, width), F32), ((qr, width), BF)],
            [vm((width // LANES, rows, LANES), F32)],
            dx1,
            both,
        )
        q_sum = rest_of_grp(q_sum)

        def from_peer(s, other):
            if not s and not other:
                return q_sum
            pairs = [
                (g * n + d, (g ^ other) * n + e) for g in range(groups) for d, e in shift(s)
            ]
            return lax.ppermute(q_sum, ("grp", "samp"), pairs)

        peers_same = [from_peer(s, 0) for s in range(hpd)]
        peers_other = [from_peer(s, 1) for s in range(hpd)]
        grad_sample_qkv, vec_sum, grad_down, grad_up, grad_fqkv, grad_fout, grad_sout, vu = call(
            functools.partial(gather_kernel, hpd),
            [
                ((piece, 3 * width), F32),
                ((8, width), F32),
                ((fpiece, width), F32),
                ((piece, hidden), F32),
                ((piece, 3 * width), F32),
                ((piece, width), F32),
                ((piece, width), F32),
                ((16, width), F32),
            ],
            [],
            r1,
            x1,
            *peers_same,
            *peers_other,
            sums,
            sums_got,
            smem=(0, 1),
        )

        def own(v):
            return lax.dynamic_slice_in_dim(v, me * (v.shape[0] // n), v.shape[0] // n, 0)

        def own_rows(v):
            return lax.dynamic_slice_in_dim(v, me * piece, piece, 1)

        five = own_rows(vu[:5])
        two = own_rows(vec_sum[:2])
        vectors = [five[i] for i in range(5)]
        vectors.append(own(vu[5 : 5 + hidden // width].reshape(-1)))
        return (
            out[None],
            grad_tokens[None],
            two[0],
            two[1],
            grad_sample_qkv,
            grad_sout,
            vectors[0],
            vectors[1],
            grad_fqkv,
            grad_fout,
            vectors[2],
            vectors[3],
            grad_up,
            vectors[5],
            grad_down,
            vectors[4],
        )

    rep = P()
    data = P("grp", "samp", None, None)
    line = P("samp")
    flat = P("samp", None)
    in_specs = (data, P("grp", "samp"), data) + (rep,) * 14
    out_specs = (
        data,
        data,
        line,
        line,
        flat,
        flat,
        line,
        line,
        flat,
        flat,
        line,
        line,
        flat,
        line,
        flat,
        line,
    )
    return jax.shard_map(body, mesh=mesh, in_specs=in_specs, out_specs=out_specs, check_vma=False)
```

time: 316 us -> 268 us (0.85)
  Pallas kernels: 130 us -> 111 us
  other arithmetic: 16.3 us -> 0 us
  local copies, waits for them, and re-layouts: 21.9 us -> 8.55 us
  between operations: 0.9 us -> 14.1 us
  waiting for transfers between devices: 72.7 us -> 65.7 us
  starting transfers between devices: 19.1 us -> 14.6 us
    ppermute x12 -> x7, waiting for transfers between devices: 72.6 us -> 9.57 us  [the longest x3 4.15 us: from_peer(): return lax.ppermute(q_sum, ('grp', 'samp'), pairs)]
    reduce_scatter x0 -> x1, waiting for transfers between devices: none -> 30.3 us  [body(): sums = lax.psum_scatter(sums, 'samp', scatter_dimension=0, tiled=True)[0]]
    pallas_call x7 -> x10, Pallas kernels: 130 us -> 111 us  [call(): pl.pallas_call(fn, out_shape=[jax.ShapeDtypeStruct(*o) for o in outs], in...]
    all_to_all x1, waiting for transfers between devices: 0.01 us -> 12.4 us  [body(): lax.all_to_all(both, 'samp', 0, 0, tiled=True, axis_index_groups=peers)]
    all_to_all x1, waiting for transfers between devices: 0.01 us -> 11.1 us  [body(): do_recv = lax.all_to_all(do_send, 'samp', 0, 0, tiled=True)]
    convert_element_type x7 -> x0, other arithmetic: 9.78 us -> none  [the longest x6 9.66 us: add(): return (a.astype(F32) + b.astype(F32)).astype(BF)]
    ppermute x12 -> x7, starting transfers between devices: 10.6 us -> 5.29 us  [the longest x2 2.92 us: swap_grp(): return lax.ppermute(v, 'grp', [(d, d ^ 1 << bit) for d in range(groups)])]
    dynamic_update_slice x2 -> x0, local copies, waits for them, and re-layouts: 3.97 us -> none  [body(): cols = lax.dynamic_update_slice(cols, give[:, :, None], (0, 0, src, 0))]
  transfers between devices with their start and end apart: 15 -> 11, of which waited for: 7 -> 9; matrix products, arithmetic and copies ran while one was open for 9% -> 0% of each run, Pallas kernels for 15% -> 18%
where the time goes in v2:
time: 268 us
  Pallas kernels  111 us (41%)
  waiting for transfers between devices  65.7 us (25%)
  blocking collectives  54 us (20%)
  starting transfers between devices  14.6 us (5%)
  between operations  14.1 us (5%)
  local copies, waits for them, and re-layouts  8.55 us (3%)
    pallas_call x10, Pallas kernels, call(): pl.pallas_call(fn, out_shape=[jax.ShapeDtypeStruct(*o) for o in outs], in...  111 us
    reduce_scatter x1, waiting for transfers between devices, body(): sums = lax.psum_scatter(sums, 'samp', scatter_dimension=0, tiled=True)[0]  30.3 us
    all_to_all x1, blocking collectives, body(): mine = lax.all_to_all(xt, 'samp', 0, 0, tiled=True, axis_index_groups=peers)  29.5 us
    all_to_all x1, blocking collectives, body(): o_recv = lax.all_to_all(o_send, 'samp', 0, 0, tiled=True)  24.5 us
    all_to_all x1, waiting for transfers between devices, body(): lax.all_to_all(both, 'samp', 0, 0, tiled=True, axis_index_groups=peers)  12.4 us
    all_to_all x1, waiting for transfers between devices, body(): do_recv = lax.all_to_all(do_send, 'samp', 0, 0, tiled=True)  11.1 us
    unnamed x24, local copies, waits for them, and re-layouts  5.85 us
    all_to_all x1, starting transfers between devices, body(): lax.all_to_all(both, 'samp', 0, 0, tiled=True, axis_index_groups=peers)  5.39 us
  transfers between devices with their start and end apart: 11, of which 9 were waited for; matrix products, arithmetic and copies ran while one was open for 0% of the time, Pallas kernels for 18%

profile of v2, /device:TPU:0, one launch (start us, length us, event | category | flops | bytes accessed | tf_op | source)
XLA Modules:
  0.0 267.7 jit_solution(5155058742628174708)
XLA Ops:
  7.2 2.5 shard_map.288.xt
  9.7 29.5 %all_to_all.20.refs_0_.refs_4_ = bf16[8,104,512]{2,1,0:T(8,128)(2,1)S(1)} all-to-all(bf16[8,104,512]{2,1,0:T(8,128)(2,1)} %shard_map.288.xt), channel_id=1, replica_groups={{0,2,4,6,8,10,12,14},{1,3,5,7,9,11,13,15},{16,18,20,22,24,26,28,30},{17..., dimensions={0} | all-to-all | bytes 1703936 | tf_op jit(solution)/shard_map/all_to_all | solution.py:902
  39.2 2.4 collective-permute-done.refs_1_
  42.5 21.5 %shard_map.289 = (bf16[16,96,256]{2,1,0:T(8,128)(2,1)}, bf16[1536,512]{1,0:T(8,128)(2,1)}, bf16[256,1536]{1,0:T(8,128)(2,1)}, f32[8,1536]{1,0:T(8,128)}, f32[8,1...) custom-call(s32[1]{0:T(128)} %bitcast.r_ref, bf16[8,104,512]{2,1,0:T(8,128)(2,1)} %copy-done, ...), custom_call_target="tpu_custom_call" | custom-call | tf_op jit(solution)/shard_map/pallas_call | solution.py:94
  64.0 24.5 %all_to_all.21.o_recv = bf16[16,96,256]{2,1,0:T(8,128)(2,1)} all-to-all(bf16[16,96,256]{2,1,0:T(8,128)(2,1)} %get-tuple-element.51), channel_id=1, replica_groups=mesh['grp'=2,'samp'=16] {'samp'}, dimensions={0} | all-to-all | bytes 1572864 | tf_op jit(solution)/shard_map/all_to_all | solution.py:939
  88.6 37.3 %shard_map.290 = (bf16[96,8,512]{2,1,0:T(8,128)(2,1)}, f32[768,512]{1,0:T(8,128)}, bf16[16,96,256]{2,1,0:T(8,128)(2,1)}, bf16[16,432,512]{2,1,0:T(8,128)(2,1)}) custom-call(bf16[16,96,256]{2,1,0:T(8,128)(2,1)} %all_to_all.21.o_recv, bf16[8,104,512]{2,1,0:T(8,128)(2,1)} %shard_map.288.xt, bf16[96,8,512]{2,1,0:T(8,128)(2,1)} %bitcast.32, f32[1,512]{1,0:T(1,128)} %bitcast.45, ...), custom_call_target="tpu_custom_call" | custom-call | tf_op jit(solution)/shard_map/pallas_call | solution.py:94
  125.9 3.9 %all-to-all-start.2 = ((bf16[16,96,256]{2,1,0:T(8,128)(2,1)}), bf16[16,96,256]{2,1,0:T(8,128)(2,1)S(1)}, u32[]{:S(2)}, u32[]{:S(2)}) async-start(bf16[16,96,256]{2,1,0:T(8,128)(2,1)} %get-tuple-element.55), calls=%async_computation.2 | async-start | bytes 1572864 | tf_op jit(solution)/shard_map/all_to_all | solution.py:990
  129.8 7.6 %shard_map.291 = (bf16[1536,256]{1,0:T(8,128)(2,1)}, bf16[1536,256]{1,0:T(8,128)(2,1)}, bf16[256,1536]{1,0:T(8,128)(2,1)}, bf16[4,128,1536]{2,1,0:T(8,128)(2,1)}, bf16[512,1536]{1,0:T(8,128)(2,1)}) custom-call(s32[1]{0:T(128)} %bitcast.r_ref, bf16[1536,512]{1,0:T(8,128)(2,1)} %get-tuple-element.56.xs, f32[1,512]{1,0:T(1,128)} %bitcast.37, ...), custom_call_target="tpu_custom_call" | custom-call | tf_op jit(solution)/shard_map/pallas_call | solution.py:94
  137.4 11.1 %all-to-all-done.2.do_recv = bf16[16,96,256]{2,1,0:T(8,128)(2,1)S(1)} async-done(((bf16[16,96,256]{2,1,0:T(8,128)(2,1)}), bf16[16,96,256]{2,1,0:T(8,128)(2,1)S(1)}, u32[]{:S(2)}, u32[]{:S(2)}) %all-to-all-start.2) | async-done | bytes 786464 | tf_op jit(solution)/shard_map/all_to_all | solution.py:990
  149.4 18.6 %shard_map.292.dt = bf16[768,1536]{1,0:T(8,128)(2,1)} custom-call(s32[1]{0:T(128)} %bitcast.r_ref, s32[8]{0:T(128)} %get-tuple-element.54.start_ref, bf16[16,96,256]{2,1,0:T(8,128)(2,1)} %copy-done.2, bf16[1536,256]{1,0:T(8,128)(2,1)} %get-tuple-element.57.k_in, bf16[1536,256]{1,0:T(8,128)(2,1)} %get-tuple-element.58.v_in, ...), custom_call_target="tpu_custom_call" | custom-call | tf_op jit(solution)/shard_map/pallas_call | solution.py:94
  168.0 6.2 %shard_map.293 = (bf16[8,64,512]{2,1,0:T(8,128)(2,1)}, bf16[8,64,512]{2,1,0:T(8,128)(2,1)}) custom-call(s32[1]{0:T(128)} %bitcast.r_ref, s32[1]{0:T(128)} %bitcast.12.x_ref, bf16[768,1536]{1,0:T(8,128)(2,1)} %shard_map.292.dt, bf16[512,1536]{1,0:T(8,128)(2,1)} %get-tuple-element.64.nt, bf16[512,1536]{1,0:T(8,128)(2,1)} %w_in.5, f32[1,512]{1,0:T(1,128)} %bitcast.38, ...), custom_call_target="tpu_custom_call" | custom-call | tf_op jit(solution)/shard_map/pallas_call | solution.py:94
  174.2 1.5 collective-permute-start.3
  175.7 6.9 %shard_map.294 = (bf16[4,96,512]{2,1,0:T(8,128)(2,1)}, bf16[4,96,512]{2,1,0:T(8,128)(2,1)}, bf16[4,96,512]{2,1,0:T(8,128)(2,1)}, bf16[4,96,512]{2,1,0:T(8,128)(2,1)}) custom-call(s32[1]{0:T(128)} %bitcast.r_ref, bf16[768,1536]{1,0:T(8,128)(2,1)} %shard_map.292.dt, bf16[512,1536]{1,0:T(8,128)(2,1)} %w_in.5, f32[1536,128]{1,0:T(8,128)} %get-tuple-element.67.rank_col), custom_call_target="tpu_custom_call" | custom-call | tf_op jit(solution)/shard_map/pallas_call | solution.py:94
  183.1 1.4 collective-permute-done.1.refs_2_
  185.1 3.4 %collective-permute-done.3.refs_7_ = bf16[8,64,512]{2,1,0:T(8,128)(2,1)S(1)} collective-permute-done((bf16[8,64,512]{2,1,0:T(8,128)(2,1)}, bf16[8,64,512]{2,1,0:T(8,128)(2,1)S(1)}, u32[]{:S(2)}, u32[]{:S(2)}) %collective-permute-start.3) | collective-permute-done | bytes 524320 | tf_op jit(solution)/shard_map/ppermute | solution.py:839
  189.3 4.2 %shard_map.295 = bf16[8,160,512]{2,1,0:T(8,128)(2,1)} custom-call(bf16[4,96,512]{2,1,0:T(8,128)(2,1)} %get-tuple-element.68.refs_0_, bf16[4,96,512]{2,1,0:T(8,128)(2,1)} %get-tuple-element.69.refs_1_, bf16[4,96,512]{2,1,0:T(8,128)(2,1)} %copy-done.6, bf16[4,96,512]{2,1,0:T(8,128)(2,1)} %copy-done.7, bf16[8,104,512]{2,1,0:T(8,128)(2,1)} %copy-done, ...), custom_call_target="tpu_custom_call" | custom-call | tf_op jit(solution)/shard_map/pallas_call | solution.py:94
  193.5 5.4 %all-to-all-start.3 = ((bf16[8,160,512]{2,1,0:T(8,128)(2,1)}), bf16[8,160,512]{2,1,0:T(8,128)(2,1)S(1)}, u32[]{:S(2)}, u32[]{:S(2)}) async-start(bf16[8,160,512]{2,1,0:T(8,128)(2,1)} %shard_map.295), calls=%async_computation.3 | async-start | bytes 2621440 | tf_op jit(solution)/shard_map/all_to_all | solution.py:1076
  198.9 30.3 %reduce-scatter.2.cloned.1.call-done = bf16[1,432,512]{2,1,0:T(8,128)(2,1)} async-done(((bf16[16,432,512]{2,1,0:T(8,128)(2,1)}), bf16[1,432,512]{2,1,0:T(8,128)(2,1)}) %reduce-scatter.2.cloned.1.call-update) | async-done | bytes 442384 | tf_op jit(solution)/shard_map/reduce_scatter | solution.py:989
  229.2 1.4 collective-permute-start.7
  230.6 12.4 %all-to-all-done.3.both = bf16[8,160,512]{2,1,0:T(8,128)(2,1)S(1)} async-done(((bf16[8,160,512]{2,1,0:T(8,128)(2,1)}), bf16[8,160,512]{2,1,0:T(8,128)(2,1)S(1)}, u32[]{:S(2)}, u32[]{:S(2)}) %all-to-all-start.3) | async-done | bytes 1310752 | tf_op jit(solution)/shard_map/all_to_all | solution.py:1076
  244.0 3.7 %shard_map.296 = (f32[96,8,512]{2,1,0:T(8,128)}, bf16[64,512]{1,0:T(8,128)(2,1)}) custom-call(f32[768,512]{1,0:T(8,128)} %get-tuple-element.73.dx1, bf16[8,160,512]{2,1,0:T(8,128)(2,1)} %copy-done.1), custom_call_target="tpu_custom_call" | custom-call | tf_op jit(solution)/shard_map/pallas_call | solution.py:94
  249.6 2.7 %collective-permute-done.6.refs_3_ = bf16[64,512]{1,0:T(8,128)(2,1)S(1)} collective-permute-done((bf16[64,512]{1,0:T(8,128)(2,1)}, bf16[64,512]{1,0:T(8,128)(2,1)S(1)}, u32[]{:S(2)}, u32[]{:S(2)}) %collective-permute-start.6) | collective-permute-done | bytes 65568 | tf_op jit(solution)/shard_map/ppermute | solution.py:1096
  252.3 1.4 collective-permute-done.5.refs_2_
  255.1 2.3 shard_map.297
  (41 shorter events, 11.5 us)
Async XLA Ops:
  7.2 222.0 %reduce-scatter.2.cloned.1.call-start = ((), (), s32[]{:S(2)}) async-start(), calls=%async_computation.5 | async-start | bytes 7520256 | tf_op jit(solution)/shard_map/reduce_scatter | solution.py:989
  39.2 2.4 copy-start
  39.2 2.4 collective-permute-start
  41.6 1.0 copy-start.3
  125.9 22.6 %all-to-all-start.2 = ((bf16[16,96,256]{2,1,0:T(8,128)(2,1)}), bf16[16,96,256]{2,1,0:T(8,128)(2,1)S(1)}, u32[]{:S(2)}, u32[]{:S(2)}) async-start(bf16[16,96,256]{2,1,0:T(8,128)(2,1)} %get-tuple-element.55), calls=%async_computation.2 | async-start | bytes 1572864 | tf_op jit(solution)/shard_map/all_to_all | solution.py:990
  148.5 0.9 copy-start.2
  174.2 14.3 %collective-permute-start.3 = (bf16[8,64,512]{2,1,0:T(8,128)(2,1)}, bf16[8,64,512]{2,1,0:T(8,128)(2,1)S(1)}, u32[]{:S(2)}, u32[]{:S(2)}) collective-permute-start(bf16[8,64,512]{2,1,0:T(8,128)(2,1)} %get-tuple-element.65), channel_id=1, source_target_pairs={{0,16},{16,0},{1,17},{17,1},{2,18},{18,2},{3,19},{19,3},{4,20},{20... | collective-permute-start | bytes 1572872 | tf_op jit(solution)/shard_map/ppermute | solution.py:839
  182.6 1.9 collective-permute-start.1
  182.6 2.5 collective-permute-start.2
  184.5 4.0 %copy-start.6 = (bf16[4,96,512]{2,1,0:T(8,128)(2,1)}, bf16[4,96,512]{2,1,0:T(8,128)(2,1)S(1)}, u32[]{:S(2)}) copy-start(bf16[4,96,512]{2,1,0:T(8,128)(2,1)S(1)} %collective-permute-done.1.refs_2_) | copy-start | bytes 1179652
  185.1 3.5 %copy-start.7 = (bf16[4,96,512]{2,1,0:T(8,128)(2,1)}, bf16[4,96,512]{2,1,0:T(8,128)(2,1)S(1)}, u32[]{:S(2)}) copy-start(bf16[4,96,512]{2,1,0:T(8,128)(2,1)S(1)} %collective-permute-done.2.refs_3_) | copy-start | bytes 1179652
  188.5 0.8 copy-start.4
  193.5 49.5 %all-to-all-start.3 = ((bf16[8,160,512]{2,1,0:T(8,128)(2,1)}), bf16[8,160,512]{2,1,0:T(8,128)(2,1)S(1)}, u32[]{:S(2)}, u32[]{:S(2)}) async-start(bf16[8,160,512]{2,1,0:T(8,128)(2,1)} %shard_map.295), calls=%async_computation.3 | async-start | bytes 2621440 | tf_op jit(solution)/shard_map/all_to_all | solution.py:1076
  229.2 24.6 %collective-permute-start.7 = (bf16[432,512]{1,0:T(8,128)(2,1)}, bf16[432,512]{1,0:T(8,128)(2,1)S(1)}, u32[]{:S(2)}, u32[]{:S(2)}) collective-permute-start(bf16[432,512]{1,0:T(8,128)(2,1)} %bitcast.34), channel_id=1, source_target_pairs={{0,16},{16,0},{1,17},{17,1},{2,18},{18,2},{3,19},{19,3},{4,20},{20... | collective-permute-start | bytes 1327112 | tf_op jit(solution)/shard_map/ppermute | solution.py:839
  242.9 1.1 copy-start.1
  247.7 4.6 %collective-permute-start.6 = (bf16[64,512]{1,0:T(8,128)(2,1)}, bf16[64,512]{1,0:T(8,128)(2,1)S(1)}, u32[]{:S(2)}, u32[]{:S(2)}) collective-permute-start(bf16[64,512]{1,0:T(8,128)(2,1)} %get-tuple-element.75.refs_0_), channel_id=1, source_target_pairs={{0,17},{1,16},{2,19},{3,18},{4,21},{5,20},{6,23},{7,22},{8,25},{9,... | collective-permute-start | bytes 196616 | tf_op jit(solution)/shard_map/ppermute | solution.py:1096
  248.5 5.2 %collective-permute-start.5 = (bf16[64,512]{1,0:T(8,128)(2,1)}, bf16[64,512]{1,0:T(8,128)(2,1)S(1)}, u32[]{:S(2)}, u32[]{:S(2)}) collective-permute-start(bf16[64,512]{1,0:T(8,128)(2,1)} %get-tuple-element.75.refs_0_), channel_id=1, source_target_pairs={{0,16},{1,17},{2,18},{3,19},{4,20},{5,21},{6,22},{7,23},{8,24},{9,... | collective-permute-start | bytes 196616 | tf_op jit(solution)/shard_map/ppermute | solution.py:1096
  249.2 4.5 %collective-permute-start.4 = (bf16[64,512]{1,0:T(8,128)(2,1)}, bf16[64,512]{1,0:T(8,128)(2,1)S(1)}, u32[]{:S(2)}, u32[]{:S(2)}) collective-permute-start(bf16[64,512]{1,0:T(8,128)(2,1)} %get-tuple-element.75.refs_0_), channel_id=1, source_target_pairs={{0,1},{1,0},{2,3},{3,2},{4,5},{5,4},{6,7},{7,6},{8,9},{9,8},{10,11... | collective-permute-start | bytes 196616 | tf_op jit(solution)/shard_map/ppermute | solution.py:1096
  252.3 1.4 copy-start.8
  253.7 0.6 copy-start.9
  253.7 0.6 copy-start.10
  254.4 0.8 copy-start.5
Sparse Core Ops, SparseCore 0:
  126.0 103.0 reduce-scatter.1
